TPU v7x, 128 devices: a whole 4x4x4 slice. The times are simulated.
128 devices in a mesh: section: 2 (over z_hi), ctx: 2 (over z_lo), fsdp: 32 (over y, x, core).
Axes of the slice: x: 4, y: 4, z: 4 (z_hi: 2, z_lo: 2; z = z_hi * 2 + z_lo), core: 2. Of those that a mesh axis runs over, the one named last changes fastest.
Arguments:
- inputs: bfloat16 [2, 32, 256, 1024], P(None, 'fsdp', 'ctx'), may hold values from -6 to 6
- cotangent: bfloat16 [2, 32, 256, 1024], P(None, 'fsdp', 'ctx'), may hold values from -6 to 6
- segments: int32 [2, 32, 256], P(None, 'fsdp'), may hold values from 0 to 3, as said below
- positions: int32 [2, 32, 256], P(None, 'fsdp', 'ctx'), may hold values from 0 to 767, as said below
- attention_gain: bfloat16 [2, 1024], P('section', 'fsdp'), may hold values from 0.5 to 1.5
- attention_bias: bfloat16 [2, 1024], P('section', 'fsdp'), may hold values from -2 to 2
- joint_weight: bfloat16 [2, 1024, 3072], P('section', 'fsdp'), may hold values from -0.1875 to 0.1875
- joint_bias: bfloat16 [2, 3072], P('section', 'fsdp'), may hold values from -2 to 2
- output_weight: bfloat16 [2, 1024, 1024], P('section', 'fsdp'), may hold values from -0.5 to 0.5
- output_bias: bfloat16 [2, 1024], P('section', 'fsdp'), may hold values from -2 to 2
- feed_gain: bfloat16 [2, 1024], P('section', 'fsdp'), may hold values from 0.5 to 1.5
- feed_bias: bfloat16 [2, 1024], P('section', 'fsdp'), may hold values from -2 to 2
- up_weight: bfloat16 [2, 1024, 4096], P('section', 'fsdp'), may hold values from -0.1875 to 0.1875
- up_bias: bfloat16 [2, 4096], P('section', 'fsdp'), may hold values from -2 to 2
- down_weight: bfloat16 [2, 4096, 1024], P('section', 'fsdp'), may hold values from -0.09375 to 0.09375
- down_bias: bfloat16 [2, 1024], P('section', 'fsdp'), may hold values from -2 to 2
Outputs:
- section_out: bfloat16 [2, 2, 32, 256, 1024], P('section', None, 'fsdp', 'ctx')
- input_grad: bfloat16 [2, 2, 32, 256, 1024], P('section', None, 'fsdp', 'ctx')
- attention_gain_grad: float32 [2, 1024], P('section', 'fsdp')
- attention_bias_grad: float32 [2, 1024], P('section', 'fsdp')
- joint_weight_grad: float32 [2, 1024, 3072], P('section', 'fsdp')
- joint_bias_grad: float32 [2, 3072], P('section', 'fsdp')
- output_weight_grad: float32 [2, 1024, 1024], P('section', 'fsdp')
- output_bias_grad: float32 [2, 1024], P('section', 'fsdp')
- feed_gain_grad: float32 [2, 1024], P('section', 'fsdp')
- feed_bias_grad: float32 [2, 1024], P('section', 'fsdp')
- up_weight_grad: float32 [2, 1024, 4096], P('section', 'fsdp')
- up_bias_grad: float32 [2, 4096], P('section', 'fsdp')
- down_weight_grad: float32 [2, 4096, 1024], P('section', 'fsdp')
- down_bias_grad: float32 [2, 1024], P('section', 'fsdp')
Inputs may be any that keep to these rules, and one draw needn't show every extreme that they name: `segments`: document numbers of a sequence start at 0 and rise by one at each new document; every sequence has the same number of documents, and its last one carries the largest number allowed; one document of every sequence holds tokens 256 / 2 - 1 and 128. Within a document positions rise by one from token to token; the last token of every sequence has position 767.
All inputs are finite; a program needn't handle non-finite values.
Results may differ from a plain program's by a relative error of at most 0.024.
Values may be sent and summed in bfloat16 or wider, within the bound.
No kernel may reach another device: no remote copies, remote signals or barrier semaphores. Data moves between devices by JAX's collectives and lax.ppermute only.
A program may use at most 192 MiB of HBM per device.

v0:
```python
import functools
import math

import jax
import jax.numpy as jnp
from jax import lax
from jax.experimental import pallas as pl
from jax.experimental.pallas import tpu as pltpu
from jax.sharding import Mesh
from jax.sharding import PartitionSpec as P

D = 1024
HEAD_DIM = 64
ROT = 16
SEQ = 256
LOCAL = 256
FEED = 1024
HERE = LOCAL // HEAD_DIM
EPSILON = 1e-05
LOW = jnp.bfloat16
FULL = jnp.float32
VMEM = 60 * 1024 * 1024


def shift(block, axis, distance):
    size = lax.axis_size(axis)
    return lax.ppermute(block, axis, [(i, (i + distance) % size) for i in range(size)])


def direct_blocks(block, axis):
    return [shift(block, axis, d) for d in (1, 2, 3)]


def stack_four(block, others, axis):
    me = lax.axis_index(axis)
    whole = jnp.zeros((4,) + block.shape, block.dtype)
    for distance, part in enumerate((block, *others)):
        whole = lax.dynamic_update_slice_in_dim(whole, part[None], (me - distance) % 4, 0)
    return whole


def shift_pair(block, axis, apart):
    size = lax.axis_size(axis)
    return lax.ppermute(block, axis, [(i, i ^ apart) for i in range(size)])


def quarter_of(block, dim, index):
    return lax.dynamic_index_in_dim(block, index % 4, dim, False)


def ring_start(block, axis, dim):
    far = quarter_of(block, dim, lax.axis_index(axis) + 2)
    cut = far.shape[-1] // 2
    return [shift(far[..., :cut], axis, 1), shift(far[..., cut:], axis, -1)]


def ring_next(block, axis, dim, up, down):
    me = lax.axis_index(axis)
    cut = up.shape[-1]
    ahead = quarter_of(block, dim, me + 1)
    behind = quarter_of(block, dim, me - 1)
    ahead = jnp.concatenate([plus(ahead[..., :cut], up), ahead[..., cut:]], -1)
    behind = jnp.concatenate([behind[..., :cut], plus(behind[..., cut:], down)], -1)
    return [shift(ahead, axis, 1), shift(behind, axis, -1)]


def direct(block, axis, dim):
    me = lax.axis_index(axis)
    return [shift(quarter_of(block, dim, me + d), axis, d) for d in (1, 3, 2)]


def together(*groups):
    flat = lax.optimization_barrier(tuple(item for group in groups for item in group))
    result = []
    for group in groups:
        result.append(flat[: len(group)])
        flat = flat[len(group) :]
    return result


def plus(*terms):
    return sum(term.astype(FULL) for term in terms).astype(LOW)


def after(block, *others):
    return lax.optimization_barrier((block,) + others)[0]


def in_order(index, own, other, dim):
    return jnp.where(
        index == 0,
        jnp.concatenate([own, other], dim),
        jnp.concatenate([other, own], dim),
    )


def pair(block, axis, dim):
    return in_order(lax.axis_index(axis), block, shift(block, axis, 1), dim)


def dot(left, right):
    return jnp.dot(left, right, preferred_element_type=FULL)


def dot_back(left, right):
    return lax.dot_general(left, right, (((1,), (1,)), ((), ())), preferred_element_type=FULL)


def dot_over(left, right):
    return lax.dot_general(left, right, (((0,), (0,)), ((), ())), preferred_element_type=FULL)


def turn(heads, cosine, sine):
    lane = lax.broadcasted_iota(jnp.int32, heads.shape, 1) % HEAD_DIM
    partner = jnp.where(
        lane < ROT // 2,
        pltpu.roll(heads, LOCAL - ROT // 2, 1),
        pltpu.roll(heads, ROT // 2, 1),
    )
    return heads * cosine + partner * sine


def normalize(hidden):
    centred = hidden - jnp.mean(hidden, -1, keepdims=True)
    scale = lax.rsqrt(jnp.mean(centred * centred, -1, keepdims=True) + EPSILON)
    return centred * scale, scale


def head_lanes(head):
    lane = lax.broadcasted_iota(jnp.int32, (SEQ, LOCAL), 1)
    return lane // HEAD_DIM == head


def head_stack(block):
    full = block.astype(FULL)
    copies = [jnp.where(head_lanes(head), full, 0.0) for head in range(HERE)]
    return jnp.concatenate(copies, 0).astype(LOW)


def head_pick(block):
    result = block[0]
    for head in range(1, HERE):
        result = jnp.where(head_lanes(head), block[head], result)
    return result


def by_head(block):
    return block.reshape(HERE, SEQ, SEQ)


def allowed_keys(seg_row, seg_col):
    query = lax.broadcasted_iota(jnp.int32, (SEQ, SEQ), 0)
    key = lax.broadcasted_iota(jnp.int32, (SEQ, SEQ), 1)
    return (seg_col == seg_row) & (query >= key)


def forward_kernel(keep, load, out, store):
    hidden, seg_row, seg_col, cosine, sine, params, w_joint, w_out, w_up, w_down = load
    normed, _ = normalize(hidden()[...].astype(FULL))
    params = params()
    first = (normed * params[0:1] + params[1:2]).astype(LOW)
    second = (normed * params[2:3] + params[3:4]).astype(LOW)
    if keep:
        out[2][...] = first
        out[3][...] = second
        store(2, 3)
    cos = jnp.concatenate([cosine()[...]] * 2, 1)
    sin = jnp.concatenate([sine()[...]] * 2, 1)
    joint = dot(first, w_joint()[...]) + params[4:5, : 3 * LOCAL]
    query = turn(joint[:, :LOCAL], cos, sin)
    keys = turn(joint[:, LOCAL : 2 * LOCAL], cos, sin).astype(LOW)
    values = joint[:, 2 * LOCAL :].astype(LOW)
    if keep:
        out[4][...] = query.astype(LOW)
        out[5][...] = keys
        out[6][...] = values
        store(4, 5, 6)
    contexts = []
    for seq in range(2):
        part = slice(seq * SEQ, seq * SEQ + SEQ)
        scores = by_head(dot_back(head_stack(query[part]), keys[part]))
        scores = jnp.where(
            allowed_keys(seg_row()[seq], seg_col()[seq])[None],
            scores * HEAD_DIM**-0.5,
            -1000000000.0,
        )
        top = jnp.max(scores, -1, keepdims=True)
        weight = jnp.exp(scores - top)
        total = jnp.sum(weight, -1, keepdims=True)
        probs = (weight * (1.0 / total)).astype(LOW).reshape(HERE * SEQ, SEQ)
        contexts.append(head_pick(by_head(dot(probs, values[part]))).astype(LOW))
        if keep:
            out[7][pl.ds(seq * HERE, HERE)] = top + jnp.log(total)
    context = jnp.concatenate(contexts, 0)
    if keep:
        out[8][...] = context
        store(7, 8)
    upward = dot(second, w_up()[...]) + params[5:6]
    half = 0.5 * (1.0 + lax.erf(upward * math.sqrt(0.5)))
    active = (upward * half).astype(LOW)
    if keep:
        out[9][...] = active
        slope = half + upward * jnp.exp(-0.5 * upward * upward) * math.sqrt(0.5 / math.pi)
        out[10][...] = slope.astype(LOW)
        store(9, 10)
    result = (dot(context, w_out()[:, :D]) + dot(active, w_down()[...])).astype(LOW)
    out[0][...] = result[:SEQ]
    out[1][...] = result[SEQ:]
    store(0, 1)


def backward_kernel(keep, load, out, store):
    (grad, w_out, seg_row, seg_col, query_in, keys_in, values_in, lse_in) = load[:8]
    (cosine, sine, params, w_joint, w_down, slope, w_up, hidden) = load[8:]
    g = grad()[...]
    context_grad = dot_back(g, w_out()[:, :D])
    turned = []
    for seq in range(2):
        part = slice(seq * SEQ, seq * SEQ + SEQ)
        query = query_in()[part]
        keys = keys_in()[part]
        values = values_in()[part]
        queries = head_stack(query)
        contexts = head_stack(context_grad[part])
        scores = by_head(dot_back(queries, keys))
        scores = jnp.where(
            allowed_keys(seg_row()[seq], seg_col()[seq])[None],
            scores * HEAD_DIM**-0.5,
            -1000000000.0,
        )
        probs = jnp.exp(scores - lse_in()[pl.ds(seq * HERE, HERE)])
        probs_grad = by_head(dot_back(contexts, values))
        scores_grad = probs * (probs_grad - jnp.sum(probs * probs_grad, -1, keepdims=True))
        scores_grad = scores_grad.astype(LOW).reshape(HERE * SEQ, SEQ)
        probs = probs.astype(LOW).reshape(HERE * SEQ, SEQ)
        query_grad = head_pick(by_head(dot(scores_grad, keys)))
        keys_grad = dot_over(scores_grad, queries)
        values_grad = dot_over(probs, contexts)
        cos = jnp.concatenate([cosine()[part]] * 2, 1)
        sin = -jnp.concatenate([sine()[part]] * 2, 1)
        turned.append(
            jnp.concatenate(
                [
                    turn(query_grad * HEAD_DIM**-0.5, cos, sin),
                    turn(keys_grad * HEAD_DIM**-0.5, cos, sin),
                    values_grad,
                ],
                1,
            ).astype(LOW)
        )
    joint_grad = jnp.concatenate(turned, 0)
    if keep:
        out[3][...] = joint_grad
        store(3)
    first_grad = dot_back(joint_grad, w_joint()[...])
    up_grad = dot_back(g, w_down()[...]) * slope()[...].astype(FULL)
    up_grad = up_grad.astype(LOW)
    if keep:
        out[2][...] = up_grad
        store(2)
    second_grad = dot_back(up_grad, w_up()[...])
    normed, scale = normalize(hidden()[...].astype(FULL))
    params = params()
    inner = first_grad * params[0:1] + second_grad * params[2:3]
    back = scale * (
        inner
        - jnp.mean(inner, -1, keepdims=True)
        - normed * jnp.mean(inner * normed, -1, keepdims=True)
    )
    result = back.astype(LOW)
    out[0][...] = result[:SEQ]
    out[1][...] = result[SEQ:]
    store(0, 1)
    if keep:
        out[4][...] = jnp.zeros(out[4].shape, FULL)
        for row, item in (
            (0, first_grad * normed),
            (1, first_grad),
            (2, second_grad * normed),
            (3, second_grad),
            (4, up_grad.astype(FULL)),
            (5, g.astype(FULL)),
            (6, joint_grad.astype(FULL)),
        ):
            out[4][row : row + 1, : item.shape[1]] = jnp.sum(item, 0, keepdims=True)
        store(4)


JOINT = slice(0, 3 * LOCAL)
UP = slice(3 * LOCAL, 3 * LOCAL + FEED)
DOWN = slice(3 * LOCAL + FEED, 3 * LOCAL + FEED + D)
TOKENS = 2 * SEQ


class Pieces:
    def __init__(self, refs):
        self.refs = refs

    def __getitem__(self, index):
        return jnp.concatenate([ref[...] for ref in self.refs], 0)[index]


def call(kernel, name, operands, shapes, flops):
    arrays = []

    def number(array):
        for place, item in enumerate(arrays):
            if item is array:
                return place
        arrays.append(array)
        return len(arrays) - 1

    views = []
    for operand in operands:
        if isinstance(operand[-1], slice):
            views.append((number(operand[0]), operand[1]))
        else:
            views.append([number(array) for array in operand])

    def body(*refs):
        sources, results = refs[: len(arrays)], refs[len(arrays) :]

        def loader(view):
            if isinstance(view, tuple):
                return lambda: sources[view[0]].at[:, view[1]]
            if len(view) == 1:
                return lambda: sources[view[0]]
            return lambda: Pieces([sources[place] for place in view])

        kernel([loader(view) for view in views], results, lambda *numbers: None)

    return pl.pallas_call(
        body,
        in_specs=[pl.BlockSpec(memory_space=pltpu.VMEM)] * len(arrays),
        out_specs=[pl.BlockSpec(memory_space=pltpu.VMEM)] * len(shapes),
        out_shape=[jax.ShapeDtypeStruct(shape, kind) for shape, kind in shapes],
        compiler_params=pltpu.CompilerParams(vmem_limit_bytes=16 * 1024 * 1024),
        cost_estimate=flops
        and pl.CostEstimate(flops=flops, bytes_accessed=8 * D * D, transcendentals=0),
        name=name,
    )(*arrays)


def own_call(kernel, name, operands, shapes, flops, early):
    arrays = []
    parts = []
    held = []
    for operand in operands:
        if isinstance(operand[-1], slice):
            array, columns = operand
            parts.append([(len(arrays), columns, None)])
            arrays.append(array)
            held.append(((array.shape[0], columns.stop - columns.start), array.dtype))
        else:
            row = 0
            pieces = []
            for array in operand:
                whole = None if len(operand) == 1 else pl.ds(row, array.shape[0])
                pieces.append((len(arrays), None, whole))
                arrays.append(array)
                row += array.shape[0]
            parts.append(pieces)
            held.append(((row,) + operand[0].shape[1:], operand[0].dtype))

    def body(*refs):
        sources, refs = refs[: len(arrays)], refs[len(arrays) :]
        results, refs = refs[: len(shapes)], refs[len(shapes) :]
        near, refs = refs[: len(held)], refs[len(held) :]
        kept, (come, go) = refs[: len(shapes)], refs[len(shapes) :]
        copies = []
        for pieces, ref in zip(parts, near):
            group = []
            for index, columns, place in pieces:
                source = sources[index] if columns is None else sources[index].at[:, columns]
                target = ref if place is None else ref.at[place]
                group.append(pltpu.make_async_copy(source, target, come.at[index]))
            copies.append(group)
        for group in copies[:early]:
            for copy in group:
                copy.start()
        done = set()

        def loader(number):
            def load():
                if number not in done:
                    done.add(number)
                    for copy in copies[number]:
                        copy.wait()
                return near[number]

            return load

        sent = []

        def store(*numbers):
            for number in numbers:
                copy = pltpu.make_async_copy(kept[number], results[number], go.at[number])
                copy.start()
                sent.append(copy)

        loaders = [loader(number) for number in range(len(held))]
        for load in loaders[:early]:
            load()
        for group in copies[early:]:
            for copy in group:
                copy.start()
        kernel(loaders, kept, store)
        for load in loaders:
            load()
        for copy in sent:
            copy.wait()

    return pl.pallas_call(
        body,
        in_specs=[pl.BlockSpec(memory_space=pltpu.HBM)] * len(arrays),
        out_specs=[pl.BlockSpec(memory_space=pltpu.HBM)] * len(shapes),
        out_shape=[jax.ShapeDtypeStruct(shape, kind) for shape, kind in shapes],
        scratch_shapes=[pltpu.VMEM(shape, kind) for shape, kind in held]
        + [pltpu.VMEM(shape, kind) for shape, kind in shapes]
        + [pltpu.SemaphoreType.DMA((len(arrays),)), pltpu.SemaphoreType.DMA((len(shapes),))],
        compiler_params=pltpu.CompilerParams(vmem_limit_bytes=VMEM),
        cost_estimate=flops
        and pl.CostEstimate(flops=flops, bytes_accessed=8 * D * D, transcendentals=0),
        name=name,
    )(*arrays)


ESTIMATE = TOKENS * 16 * D * D
HALVES = [((SEQ, D), LOW)] * 2


def forward(hidden, place, layer, keep):
    seg_row, seg_col, cosine, sine = ((item,) for item in place)
    params, weights, w_out = layer
    shapes = list(HALVES)
    if keep:
        wide = ((TOKENS, D), LOW)
        narrow = ((TOKENS, LOCAL), LOW)
        lse = ((2 * HERE, SEQ, 1), FULL)
        shapes += [wide, wide, narrow, narrow, narrow, lse, narrow, wide, wide]
    operands = (
        hidden,
        seg_row,
        seg_col,
        cosine,
        sine,
        (params,),
        (weights, JOINT),
        (w_out,),
        (weights, UP),
        (weights, DOWN),
    )
    kernel = functools.partial(forward_kernel, keep)
    return call(kernel, "layer_forward", operands, shapes, ESTIMATE)


def backward(grad, hidden, place, layer, saved, keep, alone=False):
    seg_row, seg_col, cosine, sine = ((item,) for item in place)
    params, weights, w_out = layer
    shapes = list(HALVES)
    if keep:
        shapes += [((TOKENS, FEED), LOW), ((TOKENS, 3 * LOCAL), LOW), ((8, D), FULL)]
    operands = (
        grad,
        (w_out,),
        seg_row,
        seg_col,
        *((item,) for item in saved[2:6]),
        cosine,
        sine,
        (params,),
        (weights, JOINT),
        (weights, DOWN),
        (saved[8],),
        (weights, UP),
        hidden,
    )
    kernel = functools.partial(backward_kernel, keep)
    if alone:
        return own_call(kernel, "layer_backward_alone", operands, shapes, ESTIMATE, 10)
    return call(kernel, "layer_backward", operands, shapes, ESTIMATE)


def lower_upper(lower, upper, half):
    lane = lax.broadcasted_iota(jnp.int32, lower.shape, 1)
    if half == 0:
        return jnp.where(lane < HEAD_DIM, lower, pltpu.roll(upper, HEAD_DIM, 1))
    return jnp.where(lane < HEAD_DIM, pltpu.roll(lower, HEAD_DIM, 1), upper)


def choose_kernel(place, joint, up, out):
    c, k = place[0], place[1]

    def group(ref, index):
        return ref[:, pl.ds(pl.multiple_of(index * 128, 128), 128)].astype(FULL)

    for pair_ in range(6):
        lower = group(joint, 4 * pair_ + c)
        upper = group(joint, 4 * pair_ + 2 + c)
        here = slice(pair_ * 128, pair_ * 128 + 128)
        out[k, :, here] = lower_upper(lower, upper, 0).astype(LOW)
        out[1 - k, :, here] = lower_upper(lower, upper, 1).astype(LOW)
    for pair_ in range(8):
        here = slice(3 * LOCAL + pair_ * 128, 3 * LOCAL + pair_ * 128 + 128)
        for slot, core in ((0, k), (1, 1 - k)):
            lower = group(up, 4 * pair_ + core)
            upper = group(up, 4 * pair_ + 2 + core)
            block = jnp.where(
                jnp.zeros(lower.shape, jnp.int32) + c == 0,
                lower_upper(lower, upper, 0),
                lower_upper(lower, upper, 1),
            )
            out[slot, :, here] = block.astype(LOW)


def finish_kernel(
    place, block, down_in, out_own, out_other, sums, joint, out, up, down, *rest
):
    vectors, (whole, up_all, joint_all) = rest[:8], rest[8:]

    def quarter(c, k, column):
        return block[c, 32 * k : 32 * k + 32, column : column + 128].astype(FULL)

    def vector(c, k, column):
        return sums[2 * c + k, :, column : column + 128]

    for p in range(16):
        at = p // 2 * 128
        for k in range(2):
            here = slice((2 * p + k) * 128, (2 * p + k) * 128 + 128)
            up[0, :, here] = lower_upper(quarter(0, k, at), quarter(1, k, at), p % 2)
            up_all[:, here] = lower_upper(vector(0, k, at), vector(1, k, at), p % 2)
    for t in range(12):
        at = t // 2 * 128
        for c in range(2):
            here = slice((2 * t + c) * 128, (2 * t + c) * 128 + 128)
            joint[0, :, here] = lower_upper(
                quarter(c, 0, FEED + at), quarter(c, 1, FEED + at), t % 2
            )
            joint_all[:, here] = lower_upper(vector(c, 0, at), vector(c, 1, at), t % 2)
    joint_all[:, 3 * D :] = jnp.zeros((8, 128), FULL)
    for c in range(2):
        down[0, 64 * c : 64 * c + 64] = down_in[c].astype(FULL)
    out[0] = out_own[...].astype(FULL) + out_other[...].astype(FULL)
    whole[...] = sums[0] + sums[1] + sums[2] + sums[3]
    whole[5:6] = sums[0, 5:6]
    f = place[0]

    def lanes(ref, start, width):
        first = pl.multiple_of(start // 128 * 128, 128)
        return pltpu.roll(ref[:, pl.ds(first, width)], (width - start % 128) % width, 1)

    shares = lanes(whole, f * 32, 128)
    for index, row in ((0, 0), (1, 1), (3, 5), (4, 2), (5, 3), (7, 5)):
        vectors[index][...] = shares[row : row + 1, :32]
    vectors[2][...] = lanes(joint_all, f * 96, 256)[6:7, :96]
    vectors[6][...] = up_all[4:5, pl.ds(pl.multiple_of(f * 128, 128), 128)]


def down_kernel(load, out, store):
    active, grad = load
    out[0][...] = dot_over(active()[...], grad()[...]).astype(LOW)
    store(0)


def weights_kernel(load, out, store):
    second, up_grad, context, grad, first, joint_grad = load
    one, two = out
    up = dot_over(second()[...], up_grad()[...]).astype(LOW)
    one[:, :SPLIT] = up[:, :SPLIT]
    two[:, : FEED - SPLIT] = up[:, SPLIT:]
    term = dot_over(context()[...], grad()[...]).astype(LOW)
    for y in range(4):
        for x in range(4):
            rows = slice((4 * y + x) * 64, (4 * y + x) * 64 + 64)
            one[rows, SPLIT:] = term[64 * y : 64 * y + 64, LOCAL * x : LOCAL * x + LOCAL]
    store(0)
    two[:, FEED - SPLIT :] = dot_over(first()[...], joint_grad()[...]).astype(LOW)
    store(1)


SPLIT = 768


def simple_call(kernel, name, operands, shapes, scalars=0, scratch=()):
    return pl.pallas_call(
        kernel,
        in_specs=[pl.BlockSpec(memory_space=pltpu.SMEM)] * scalars
        + [pl.BlockSpec(memory_space=pltpu.VMEM)] * (len(operands) - scalars),
        out_specs=[pl.BlockSpec(memory_space=pltpu.VMEM)] * len(shapes),
        out_shape=[jax.ShapeDtypeStruct(shape, kind) for shape, kind in shapes],
        scratch_shapes=[pltpu.VMEM(shape, FULL) for shape in scratch],
        compiler_params=pltpu.CompilerParams(vmem_limit_bytes=24 * 1024 * 1024),
        name=name,
    )(*operands)


SMALL = (32, 32, 96, 32, 32, 32, 128, 32)
EDGES = [sum(SMALL[:i]) for i in range(len(SMALL) + 1)]


def choose_columns(joint_weight, up_weight):
    c = lax.axis_index("ctx")
    k = lax.axis_index("core")
    (chosen,) = simple_call(
        choose_kernel,
        "choose_columns",
        (jnp.stack([c, k]), joint_weight, up_weight),
        [((2, 32, 3 * LOCAL + FEED), LOW)],
        1,
    )
    return in_order(k, chosen[0], shift(chosen[1], "core", 1), 0)


def fetch_layer(block, tokens, small, output_weight, down_weight):
    c = lax.axis_index("ctx")
    k = lax.axis_index("core")
    quarter = 2 * c + k
    down = lax.dynamic_slice_in_dim(down_weight, c * 64, 64, 0)
    block = jnp.concatenate([block, down], 1)
    weights = lax.all_gather(block, ("y", "x"), axis=0, tiled=True)
    vectors = jnp.concatenate(small + (jnp.zeros((512 - sum(SMALL),), LOW),)).reshape(4, 128)
    vectors = jnp.concatenate([vectors, jnp.zeros((28, 128), LOW)], 0)
    mixed = pair(after(jnp.concatenate([output_weight, vectors], 1), block), "core", 0)
    others, (got,) = together(direct_blocks(mixed, "x"), [shift(tokens[0], "ctx", 1)])
    later, got = lax.optimization_barrier((tokens[1], got))
    inputs = in_order(c, tokens[0], got, 1)
    mixed = stack_four(mixed, others, "x")
    out = lax.dynamic_index_in_dim(mixed, quarter, 0, False)[:, :D]
    vectors = mixed[:, :, D:].reshape(4, 2, 32, 128)[:, :, :8].reshape(64, 128)
    out = jnp.concatenate([out, vectors], 1)
    others, (inputs_other, got) = together(
        direct_blocks(out, "y"), [shift(inputs, "core", 1), shift(later, "ctx", 1)]
    )
    cotangent = in_order(c, later, got, 1)
    out = stack_four(out, others, "y")
    inputs = (inputs, inputs_other)
    cotangent = (cotangent, shift(cotangent, "core", 1))
    vectors = out[:, :, D:].reshape(32, 8, 128)[:, :4].reshape(32, 512)
    small = [vectors[:, a:b].reshape(-1).astype(FULL) for a, b in zip(EDGES, EDGES[1:])]
    joint_bias = lax.dynamic_index_in_dim(
        small[2].reshape(3, 4, 4, HEAD_DIM), quarter, 2, False
    ).reshape(-1)
    up_bias = small[6].reshape(16, 2, 2, HEAD_DIM)
    up_bias = lax.dynamic_index_in_dim(
        lax.dynamic_index_in_dim(up_bias, c, 2, False), k, 1, False
    ).reshape(-1)
    params = jnp.stack(
        [
            small[0],
            small[1],
            small[4],
            small[5],
            jnp.pad(joint_bias, (0, D - 3 * LOCAL)),
            up_bias,
            small[3] + small[7],
            jnp.zeros((D,), FULL),
        ]
    )
    layer = (params, weights, out.reshape(LOCAL, D + 128))
    return layer, inputs, cotangent


def return_layer(one, two, down, sums, beside, late):
    c = lax.axis_index("ctx")
    k = lax.axis_index("core")
    x = lax.axis_index("x")
    y = lax.axis_index("y")
    one = one.reshape(4, 4, 64, -1)
    two = two.reshape(4, 4, 64, -1)
    sums = sums + shift_pair(sums, "y", 1)
    ones, twos, (more, beside, core) = together(
        ring_start(one, "y", 0),
        ring_start(two, "x", 1),
        [shift_pair(sums, "y", 2), beside, late[1]],
    )
    sums = sums + more
    own, give = halves_of(late[0], core)
    ones, twos, (more, got) = together(
        ring_next(one, "y", 0, *ones),
        ring_next(two, "x", 1, *twos),
        [shift_pair(sums, "x", 1), shift(give, "ctx", 1)],
    )
    sums = sums + more
    one = plus(quarter_of(one, 0, y), *ones)
    two = plus(quarter_of(two, 1, x), *twos)
    out = one[:, :, SPLIT :].transpose(1, 0, 2).reshape(1, 64, D)
    out = jnp.where(
        jnp.arange(4)[:, None, None] == 2 * c + k, out, jnp.zeros_like(out)
    )
    one = jnp.concatenate([one[:, :, : SPLIT], out], -1)
    ones, twos, (more, down_more) = together(
        direct(one, "x", 0),
        direct(two, "y", 0),
        [shift_pair(sums, "x", 2), shift(down, "ctx", 1)],
    )
    sums = sums + more
    one = plus(quarter_of(one, 0, x), *ones)
    two = plus(quarter_of(two, 0, y), *twos)
    both = jnp.concatenate([one[:, :SPLIT], two, one[:, SPLIT:]], 1)
    both = both.reshape(2, 32, -1)
    width = FEED + 3 * LOCAL
    mine = take(both, k, 0)
    (other,), (more,) = together(
        [shift(take(both, 1 - k, 0), "core", 1)], [shift(sums, "core", 1)]
    )
    sums = in_order(k, sums[None], more[None], 0)
    block = in_order(k, mine[:, :width], other[:, :width], 0)
    out = plus(mine[:, width:], other[:, width:])
    (block_more, out_more, sums_more), _ = together(
        [shift(block, "ctx", 1), shift(out, "ctx", 1), shift(sums, "ctx", 1)], [beside]
    )
    place = (4 * y + x) * 2 + k
    vectors = [((1, width), FULL) for width in SMALL]
    joint, out, up, down, *vectors = simple_call(
        finish_kernel,
        "finish",
        (
            place[None],
            in_order(c, block[None], block_more[None], 0),
            in_order(c, down[None], down_more[None], 0),
            out,
            out_more,
            in_order(c, sums, sums_more, 0),
        ),
        [((1, 32, 3 * D), FULL), ((1, 32, D), FULL), ((1, 32, 4 * D), FULL), ((1, 128, D), FULL)]
        + vectors,
        1,
        ((8, D), (8, 4 * D), (8, 3 * D + 128)),
    )
    return joint, out, up, down, vectors, beside, own + got.astype(FULL)


def plus_full(left, right):
    return left.astype(FULL) + right.astype(FULL)


def take(block, index, dim):
    return lax.dynamic_index_in_dim(block, index, dim, False)


def halves_of(mine, other):
    c = lax.axis_index("ctx")
    total = plus_full(mine, other)
    total = total.reshape(total.shape[:-2] + (2, SEQ // 2, D))
    dim = total.ndim - 3
    return take(total, c, dim), take(total, 1 - c, dim).astype(LOW)


def sum_cores(mine, other):
    return halves_of(mine, shift(other, "core", 1))


def send_on(block):
    same = lax.ppermute(block, ("section", "ctx"), [(i, (i + 2) % 4) for i in range(4)])
    flip = lax.ppermute(block, ("section", "ctx"), [(i, 3 - i) for i in range(4)])
    return same, flip


def join(keep, whole, same, flip):
    mine = jnp.where(keep, whole, in_order(lax.axis_index("ctx"), same, flip, 0))
    return mine, shift(mine, "core", 1)


def split_two(results):
    return results[0], results[1], results[2:]


def shards(
    inputs,
    cotangent,
    segments,
    positions,
    attention_gain,
    attention_bias,
    joint_weight,
    joint_bias,
    output_weight,
    output_bias,
    feed_gain,
    feed_bias,
    up_weight,
    up_bias,
    down_weight,
    down_bias,
):
    section = lax.axis_index("section")
    count = inputs.shape[0]
    block = choose_columns(joint_weight[0], up_weight[0])
    pos = pair(after(positions[:, 0], block), "ctx", 1)
    pos = jnp.stack([pos, shift(pos, "core", 1)], 1)
    seg = after(segments[:, 0], block)
    seg = jnp.stack([seg, shift(seg, "core", 1)], 1)
    early, pos, seg = lax.optimization_barrier((inputs[:, 0], pos, seg))
    layer, whole_in, whole_grad = fetch_layer(
        block,
        (early, cotangent[:, 0]),
        (
            attention_gain[0],
            attention_bias[0],
            joint_bias[0],
            output_bias[0],
            feed_gain[0],
            feed_bias[0],
            up_bias[0],
            down_bias[0],
        ),
        output_weight[0],
        down_weight[0],
    )
    bias = layer[0][6]
    lane = jnp.arange(128) % HEAD_DIM
    rates = jnp.where(lane < ROT, 10000.0 ** (-2.0 * (lane % (ROT // 2)).astype(FULL) / ROT), 0.0)
    angle = pos.astype(FULL)[..., None] * rates
    cosine = jnp.cos(angle).reshape(count, TOKENS, 128)
    sine = (jnp.sin(angle) * jnp.where(lane < ROT // 2, -1.0, 1.0)).reshape(count, TOKENS, 128)
    places = [(seg[m][:, None, :], seg[m][:, :, None], cosine[m], sine[m]) for m in range(count)]
    c = lax.axis_index("ctx")

    def of(pair_, m):
        return tuple(item[m] for item in pair_)

    def own_tokens(whole):
        return take(whole.reshape(2, SEQ // 2, D), c, 0).astype(FULL)

    def over_ctx(base, own, give):
        return (base + own + shift(give, "ctx", 1).astype(FULL)).astype(LOW)

    own_in = inputs[:, 0].astype(FULL) + bias
    part = forward(of(whole_in, 0), places[0], layer, False)
    own, give = sum_cores(*part)
    a, b = of(whole_in, 1)
    part = forward((after(a, give), b), places[1], layer, False)
    result = over_ctx(own_in[0], own, give)
    sent = [send_on(result)]
    own, give = sum_cores(part[0], after(part[1], result))
    result = over_ctx(own_in[1], own, give)
    sent.append(send_on(result))
    own_grad = cotangent[:, 0].astype(FULL)
    same, flip, _ = lax.optimization_barrier((*sent[0], result))
    hidden = [join(section == 0, whole_in[0][0], same, flip)]
    *out_zero, saved_zero = split_two(forward(hidden[0], places[0], layer, True))
    part = backward(of(whole_grad, 0), hidden[0], places[0], layer, saved_zero, False)
    own, give = sum_cores(*part)
    same, flip, _ = lax.optimization_barrier((*sent[1], part[0]))
    a, b = join(section == 0, whole_in[0][1], same, flip)
    hidden.append((a, after(b, give)))
    *out_one, saved_one = split_two(forward(hidden[1], places[1], layer, True))
    got = after(shift(give, "ctx", 1), out_one[0])
    result = (own_grad[0] + own + got.astype(FULL)).astype(LOW)
    sent = [send_on(result)]
    a, b = of(whole_grad, 1)
    part = backward((after(a, result), b), hidden[1], places[1], layer, saved_one, False)
    same, flip, *part = lax.optimization_barrier((*sent[0], *part))
    a, b = join(section == 1, whole_grad[0][0], same, flip)
    own, give = sum_cores(*part)
    result = over_ctx(own_grad[1], own, give)
    sent.append(send_on(result))
    saved = [saved_zero, saved_one]
    grads = [(a, after(b, result))]

    def last(m):
        return backward(grads[m], hidden[m], places[m], layer, saved[m], True, m == 1)

    *part_zero, up_zero, joint_zero, sums_zero = last(0)
    same, flip, part_zero[0] = lax.optimization_barrier((*sent[1], part_zero[0]))
    grads.append(join(section == 1, whole_grad[0][1], same, flip))
    both = (*grads[0], *grads[1])
    (down,) = call(
        down_kernel,
        "down_gradient",
        ((saved_zero[7], saved_one[7]), both),
        [((FEED, D), LOW)],
        None,
    )
    down_share = lax.psum_scatter(down, ("y", "x"), scatter_dimension=0, tiled=True)
    ready = grads[1][1]
    outs = [
        jnp.stack([out_zero[i], out_one[i], after(part_zero[i], ready)]) for i in range(2)
    ]
    grads[1] = (grads[1][0], after(grads[1][1], down))
    *part_one, up_one, joint_one, sums_one = last(1)
    own_early, give = sum_cores(*outs)
    one, two = own_call(
        weights_kernel,
        "weight_gradients",
        (
            (saved_zero[1], saved_one[1]),
            (up_zero, up_one),
            (saved_zero[6], saved_one[6]),
            (after(both[0], give), *both[1:]),
            (saved_zero[0], saved_one[0]),
            (joint_zero, joint_one),
        ),
        [((D, SPLIT + LOCAL), LOW), ((D, FEED - SPLIT + 3 * LOCAL), LOW)],
        None,
        2,
    )
    joint_grad, out_grad, up_grad, down_grad, small, got, late = return_layer(
        one,
        two,
        down_share,
        sums_zero + sums_one,
        shift(give, "ctx", 1),
        (part_one[0], shift(part_one[1], "core", 1)),
    )
    base = jnp.stack(
        [own_tokens(hidden[0][0]) + bias, own_tokens(hidden[1][0]) + bias, own_tokens(grads[0][0])]
    )
    early = (base + own_early + got.astype(FULL)).astype(LOW)
    late = (own_tokens(grads[1][0])[None] + late).astype(LOW)
    section_out = early[None, :2, None]
    input_grad = jnp.concatenate([early[2:], late])[None, :, None]
    return (
        section_out,
        input_grad,
        small[0],
        small[1],
        joint_grad,
        small[2],
        out_grad,
        small[3],
        small[4],
        small[5],
        up_grad,
        small[6],
        down_grad,
        small[7],
    )


def solution(mesh):
    finer = Mesh(mesh.devices.reshape(2, 2, 4, 4, 2), ("section", "ctx", "y", "x", "core"))
    fsdp = ("y", "x", "core")
    vector = P("section", fsdp)
    matrix = P("section", fsdp, None)
    tokens = P(None, fsdp, "ctx", None)
    kept = P("section", None, fsdp, "ctx", None)
    params = (
        vector,
        vector,
        matrix,
        vector,
        matrix,
        vector,
        vector,
        vector,
        matrix,
        vector,
        matrix,
        vector,
    )
    return jax.shard_map(
        shards,
        mesh=finer,
        in_specs=(tokens, tokens, P(None, fsdp, None), P(None, fsdp, "ctx")) + params,
        out_specs=(kept, kept) + params,
        check_vma=False,
    )
```

profile of v0, /device:TPU:1, one launch (start us, length us, event | category | flops | bytes accessed | tf_op | source)
XLA Modules:
  0.0 339.1 jit_solution(11069691918356845165)
XLA Ops:
  10.1 1.5 collective-permute-start
  13.8 1.8 collective-permute-start.1
  18.7 1.8 collective-permute-start.8
  20.5 1.9 fusion.7
  24.3 2.5 collective-permute-start.7
  28.0 4.2 %collective-permute-done.7 = bf16[64,1152]{1,0:T(8,128)(2,1)S(1)} collective-permute-done((bf16[64,1152]{1,0:T(8,128)(2,1)S(1)}, bf16[64,1152]{1,0:T(8,128)(2,1)S(1)}, u32[]{:S(2)}, u32[]{:S(2)}) %collective-permute-start.7) | collective-permute-done | bytes 147488 | tf_op jit(solution)/shard_map/ppermute | solution.py:27
  32.3 3.2 collective-permute-done.6
  35.5 4.6 %collective-permute-done.5 = bf16[64,1152]{1,0:T(8,128)(2,1)S(1)} collective-permute-done((bf16[64,1152]{1,0:T(8,128)(2,1)S(1)}, bf16[64,1152]{1,0:T(8,128)(2,1)S(1)}, u32[]{:S(2)}, u32[]{:S(2)}) %collective-permute-start.5) | collective-permute-done | bytes 147488 | tf_op jit(solution)/shard_map/ppermute | solution.py:27
  42.3 3.2 collective-permute-start.10
  45.9 2.7 collective-permute-start.11
  50.0 2.8 collective-permute-done.9
  56.7 21.8 %all-gather.2.cloned.1.call-done.refs_7_.refs_12_.refs_13_.refs_15_ = bf16[1024,2816]{1,0:T(8,128)(2,1)} async-done(((bf16[64,2816]{1,0:T(8,128)(2,1)}), bf16[1024,2816]{1,0:T(8,128)(2,1)}) %all-gather.2.cloned.1.call-update) | async-done | bytes 5767184 | tf_op jit(solution)/shard_map/all_gather | solution.py:621
  80.4 2.6 copy-done.46
  83.0 6.8 %layer_forward.4 = (bf16[256,1024]{1,0:T(8,128)(2,1)S(1)}, bf16[256,1024]{1,0:T(8,128)(2,1)}) custom-call(bf16[256,1024]{1,0:T(8,128)(2,1)S(1)} %get-tuple-element.270.refs_0_, bf16[256,1024]{1,0:T(8,128)(2,1)S(1)} %get-tuple-element.276.refs_1_, s32[2,1,256]{2,1,0:T(1,128)S(1)} %get-tuple-element.310.refs_2_.refs_3_, ...), custom_call_target="tpu_custom_call" | custom-call | flops 8589934592 | bytes 8388608 | tf_op jit(solution)/shard_map/layer_forward/pallas_call | solution.py:332
  92.5 1.5 collective-permute-start.15
  94.0 2.6 copy-done.47
  96.6 6.0 %layer_forward.5 = (bf16[256,1024]{1,0:T(8,128)(2,1)S(1)}, bf16[256,1024]{1,0:T(8,128)(2,1)S(1)}) custom-call(bf16[256,1024]{1,0:T(8,128)(2,1)S(1)} %get-tuple-element.150.refs_0_, bf16[256,1024]{1,0:T(8,128)(2,1)S(1)} %get-tuple-element.275.refs_1_, s32[2,1,256]{2,1,0:T(1,128)S(1)} %get-tuple-element.309.refs_2_.refs_3_, ...), custom_call_target="tpu_custom_call" | custom-call | flops 8589934592 | bytes 8388608 | tf_op jit(solution)/shard_map/layer_forward/pallas_call | solution.py:332
  103.5 2.6 maximum_select_fusion.1
  108.6 2.7 collective-permute-start.17
  111.7 4.1 %collective-permute-done.19 = bf16[128,1024]{1,0:T(8,128)(2,1)S(1)} collective-permute-done((bf16[128,1024]{1,0:T(8,128)(2,1)S(1)}, bf16[128,1024]{1,0:T(8,128)(2,1)S(1)}, u32[]{:S(2)}, u32[]{:S(2)}) %collective-permute-start.19) | collective-permute-done | bytes 262176 | tf_op jit(solution)/shard_map/ppermute | solution.py:27
  117.8 5.3 %collective-permute-done.16 = bf16[128,1024]{1,0:T(8,128)(2,1)} collective-permute-done((bf16[128,1024]{1,0:T(8,128)(2,1)S(1)}, bf16[128,1024]{1,0:T(8,128)(2,1)}, u32[]{:S(2)}, u32[]{:S(2)}) %collective-permute-start.16) | collective-permute-done | bytes 262176 | tf_op jit(solution)/shard_map/ppermute | solution.py:755
  123.1 2.4 broadcast_select_fusion.4
  126.8 2.4 fusion.51
  130.5 3.2 collective-permute-start.21
  133.9 2.6 copy-done.48
  136.5 6.2 %layer_forward.6 = (bf16[256,1024]{1,0:T(8,128)(2,1)S(1)}, bf16[256,1024]{1,0:T(8,128)(2,1)S(1)}, bf16[512,1024]{1,0:T(8,128)(2,1)S(1)}, bf16[512,1024]{1,0:T(8,...) custom-call(bf16[256,1024]{1,0:T(8,128)(2,1)S(1)} %get-tuple-element, ...), custom_call_target="tpu_custom_call" | custom-call | flops 8589934592 | bytes 8388608 | tf_op jit(solution)/shard_map/layer_forward/pallas_call | solution.py:332
  146.3 7.0 %layer_backward.3 = (bf16[256,1024]{1,0:T(8,128)(2,1)S(1)}, bf16[256,1024]{1,0:T(8,128)(2,1)S(1)}) custom-call(bf16[256,1024]{1,0:T(8,128)(2,1)S(1)} %get-tuple-element.266.refs_0_, bf16[256,1024]{1,0:T(8,128)(2,1)S(1)} %get-tuple-element.274.refs_1_, bf16[256,1152]{1,0:T(8,128)(2,1)S(1)} %bitcast.240, s32[2,1,256]{2,1,0:T(1,128)S(1)} %get-tuple-element.310.refs_2_.refs_3_, ...), custom_call_target="tpu_custom_call" | custom-call | flops 8589934592 | bytes 8388608 | tf_op jit(solution)/shard_map/layer_backward/pallas_call | solution.py:332
  158.0 6.3 %layer_forward.7 = (bf16[256,1024]{1,0:T(8,128)(2,1)S(1)}, bf16[256,1024]{1,0:T(8,128)(2,1)S(1)}, bf16[512,1024]{1,0:T(8,128)(2,1)S(1)}, bf16[512,1024]{1,0:T(8,...) custom-call(bf16[256,1024]{1,0:T(8,128)(2,1)S(1)} %get-tuple-element, ...), custom_call_target="tpu_custom_call" | custom-call | flops 8589934592 | bytes 8388608 | tf_op jit(solution)/shard_map/layer_forward/pallas_call | solution.py:332
  167.2 2.8 collective-permute-start.28
  170.2 7.9 %layer_backward.4 = (bf16[256,1024]{1,0:T(8,128)(2,1)S(1)}, bf16[256,1024]{1,0:T(8,128)(2,1)}) custom-call(bf16[256,1024]{1,0:T(8,128)(2,1)S(1)} %get-tuple-element.169.refs_0_, bf16[256,1024]{1,0:T(8,128)(2,1)S(1)} %get-tuple-element.273.refs_1_, bf16[256,1152]{1,0:T(8,128)(2,1)S(1)} %bitcast.242, s32[2,1,256]{2,1,0:T(1,128)S(1)} %get-tuple-element.309.refs_2_.refs_3_, ...), custom_call_target="tpu_custom_call" | custom-call | flops 8589934592 | bytes 8388608 | tf_op jit(solution)/shard_map/layer_backward/pallas_call | solution.py:332
  178.9 2.7 collective-permute-done.28
  184.3 2.6 broadcast_select_fusion.2
  187.0 1.5 convert_add_fusion.4
  188.7 7.1 %collective-permute-done.30 = bf16[128,1024]{1,0:T(8,128)(2,1)S(1)} collective-permute-done((bf16[128,1024]{1,0:T(8,128)(2,1)S(1)}, bf16[128,1024]{1,0:T(8,128)(2,1)S(1)}, u32[]{:S(2)}, u32[]{:S(2)}) %collective-permute-start.30) | collective-permute-done | bytes 262176 | tf_op jit(solution)/shard_map/ppermute | solution.py:27
  195.9 2.7 collective-permute-start.32
  199.1 2.6 copy-done.49
  201.7 7.4 %layer_backward.5 = (bf16[256,1024]{1,0:T(8,128)(2,1)S(1)}, bf16[256,1024]{1,0:T(8,128)(2,1)S(1)}, bf16[512,1024]{1,0:T(8,128)(2,1)S(1)}, bf16[512,768]{1,0:T(8,128)(2,1)S(1)}, f32[8,1024]{1,0:T(8,128)S(1)}) custom-call(bf16[256,1024]{1,0:T(8,128)(2,1)S(1)} %get-tuple-element.201.refs_0_.refs_2_.refs_6_, ...), custom_call_target="tpu_custom_call" | custom-call | flops 8589934592 | bytes 8388608 | tf_op jit(solution)/shard_map/layer_backward/pallas_call | solution.py:332
  209.6 2.8 broadcast_select_fusion.1
  212.5 1.7 collective-permute-start.34
  214.2 1.5 collective-permute-done.34.refs_5_.refs_1_.refs_9_
  215.8 1.4 pad_maximum_fusion
  218.0 3.7 %down_gradient.1 = bf16[1024,1024]{1,0:T(8,128)(2,1)} custom-call(bf16[512,1024]{1,0:T(8,128)(2,1)S(1)} %get-tuple-element.195.refs_0_, bf16[512,1024]{1,0:T(8,128)(2,1)S(1)} %copy-done.12, bf16[256,1024]{1,0:T(8,128)(2,1)S(1)} %get-tuple-element.201.refs_0_.refs_2_.refs_6_, bf16[256,1024]{1,0:T(8,128)(2,1)S(1)} %collective-permute-done.33.refs_1_.refs_3_.refs_7_, ...), custom_call_target="tpu_custom_call" | custom-call | tf_op jit(solution)/shard_map/down_gradient/pallas_call | solution.py:332
  221.7 12.0 %layer_backward_alone.1 = (bf16[256,1024]{1,0:T(8,128)(2,1)}, bf16[256,1024]{1,0:T(8,128)(2,1)}, bf16[512,1024]{1,0:T(8,128)(2,1)}, bf16[512,768]{1,0:T(8,128)(2,1)}, f32[8,1024]{1,0:T(8,128)}) custom-call(bf16[256,1024]{1,0:T(8,128)(2,1)} %copy-done.3, bf16[256,1024]{1,0:T(8,128)(2,1)} %copy-done.5, bf16[256,1152]{1,0:T(8,128)(2,1)} %bitcast.243, ...), custom_call_target="tpu_custom_call" | custom-call | flops 8589934592 | bytes 8388608 | tf_op jit(solution)/shard_map/layer_backward_alone/pallas_call | solution.py:413
  237.5 2.7 collective-permute-start.41
  240.2 2.0 convert_add_fusion
  242.2 1.7 copy-done.68
  244.6 9.9 %weight_gradients.1 = (bf16[1024,1024]{1,0:T(8,128)(2,1)}, bf16[1024,1024]{1,0:T(8,128)(2,1)}) custom-call(bf16[512,1024]{1,0:T(8,128)(2,1)} %copy-done.7, bf16[512,1024]{1,0:T(8,128)(2,1)} %copy-done.9, bf16[512,1024]{1,0:T(8,128)(2,1)} %copy-done.10, bf16[512,1024]{1,0:T(8,128)(2,1)} %get-tuple-element.198.refs_3_, bf16[512,256]{1,0:T(8,128)(2,1)} %copy-done.29, ...), custom_call_target="tpu_custom_call" | custom-call | tf_op jit(solution)/shard_map/weight_gradients/pallas_call | solution.py:413
  254.5 1.8 constant_dynamic-slice_fusion
  261.7 2.5 collective-permute-done.37
  264.2 2.3 collective-permute-done.36
  268.8 2.4 collective-permute-start.45
  271.3 1.4 collective-permute-start.46
  272.9 1.4 collective-permute-start.47
  274.5 1.4 collective-permute-start.49
  277.3 3.1 collective-permute-done.49
  280.4 1.5 collective-permute-done.44
  281.9 2.7 collective-permute-done.46
  287.9 1.6 collective-permute-start.55
  292.0 1.5 collective-permute-start.52
  294.1 2.6 collective-permute-start.51
  296.7 13.7 %reduce-scatter.2.cloned.1.call-done = bf16[64,1024]{1,0:T(8,128)(2,1)} async-done(((bf16[1024,1024]{1,0:T(8,128)(2,1)}), bf16[64,1024]{1,0:T(8,128)(2,1)}) %reduce-scatter.2.cloned.1.call-update) | async-done | bytes 131088 | tf_op jit(solution)/shard_map/reduce_scatter | solution.py:876
  315.7 2.4 collective-permute-start.59
  325.4 5.1 %collective-permute-done.60 = bf16[64,1792]{1,0:T(8,128)(2,1)S(1)} collective-permute-done((bf16[64,1792]{1,0:T(8,128)(2,1)S(1)}, bf16[64,1792]{1,0:T(8,128)(2,1)S(1)}, u32[]{:S(2)}, u32[]{:S(2)}) %collective-permute-start.60) | collective-permute-done | bytes 229408 | tf_op jit(solution)/shard_map/ppermute | solution.py:27
  330.6 1.4 finish.1
  (451 shorter events, 80.8 us)
Async XLA Ops:
  7.3 71.2 %all-gather.2.cloned.1.call-start = ((), (), s32[]{:S(2)}) async-start(), calls=%async_computation.1 | async-start | bytes 6127616 | tf_op jit(solution)/shard_map/all_gather | solution.py:621
  10.1 2.5 collective-permute-start
  13.4 297.0 %reduce-scatter.2.cloned.1.call-start = ((), (), s32[]{:S(2)}) async-start(), calls=%async_computation.2 | async-start | bytes 2228224 | tf_op jit(solution)/shard_map/reduce_scatter | solution.py:876
  13.8 2.8 collective-permute-start.1
  15.6 2.2 collective-permute-start.3
  16.3 8.0 %collective-permute-start.4 = (bf16[32,1152]{1,0:T(8,128)(2,1)S(1)}, bf16[32,1152]{1,0:T(8,128)(2,1)S(1)}, u32[]{:S(2)}, u32[]{:S(2)}) collective-permute-start(bf16[32,1152]{1,0:T(8,128)(2,1)S(1)} %fusion.45), channel_id=1, source_target_pairs={{0,1},{1,0},{2,3},{3,2},{4,5},{5,4},{6,7},{7,6},{8,9},{9,8},{10,11... | collective-permute-start | bytes 221192 | tf_op jit(solution)/shard_map/ppermute | solution.py:27
  16.6 2.1 collective-permute-start.2
  18.7 21.5 %collective-permute-start.8 = (bf16[2,128,1024]{2,1,0:T(8,128)(2,1)S(1)}, bf16[2,128,1024]{2,1,0:T(8,128)(2,1)S(1)}, u32[]{:S(2)}, u32[]{:S(2)}) collective-permute-start(bf16[2,128,1024]{2,1,0:T(8,128)(2,1)S(1)} %bitcast.281), channel_id=1, source_target_pairs={{0,32},{32,0},{1,33},{33,1},{2,34},{34,2},{3,35},{35,3},{4,36},{36... | collective-permute-start | bytes 1572872 | tf_op jit(solution)/shard_map/ppermute | solution.py:27
  24.3 8.0 %collective-permute-start.7 = (bf16[64,1152]{1,0:T(8,128)(2,1)S(1)}, bf16[64,1152]{1,0:T(8,128)(2,1)S(1)}, u32[]{:S(2)}, u32[]{:S(2)}) collective-permute-start(bf16[64,1152]{1,0:T(8,128)(2,1)S(1)} %maximum_select_fusion.11), channel_id=1, source_target_pairs={{0,6},{2,0},{4,2},{6,4},{1,7},{3,1},{5,3},{7,5},{8,14},{10,8},{12,... | collective-permute-start | bytes 442376 | tf_op jit(solution)/shard_map/ppermute | solution.py:27
  26.8 8.7 %collective-permute-start.6 = (bf16[64,1152]{1,0:T(8,128)(2,1)S(1)}, bf16[64,1152]{1,0:T(8,128)(2,1)S(1)}, u32[]{:S(2)}, u32[]{:S(2)}) collective-permute-start(bf16[64,1152]{1,0:T(8,128)(2,1)S(1)} %maximum_select_fusion.11), channel_id=1, source_target_pairs={{0,4},{2,6},{4,0},{6,2},{1,5},{3,7},{5,1},{7,3},{8,12},{10,14},{12... | collective-permute-start | bytes 442376 | tf_op jit(solution)/shard_map/ppermute | solution.py:27
  27.4 12.8 %collective-permute-start.5 = (bf16[64,1152]{1,0:T(8,128)(2,1)S(1)}, bf16[64,1152]{1,0:T(8,128)(2,1)S(1)}, u32[]{:S(2)}, u32[]{:S(2)}) collective-permute-start(bf16[64,1152]{1,0:T(8,128)(2,1)S(1)} %maximum_select_fusion.11), channel_id=1, source_target_pairs={{0,2},{2,4},{4,6},{6,0},{1,3},{3,5},{5,7},{7,1},{8,10},{10,12},{12... | collective-permute-start | bytes 442376 | tf_op jit(solution)/shard_map/ppermute | solution.py:27
  40.2 12.9 %collective-permute-start.13 = (bf16[2,128,1024]{2,1,0:T(8,128)(2,1)}, bf16[2,128,1024]{2,1,0:T(8,128)(2,1)S(1)}, u32[]{:S(2)}, u32[]{:S(2)}) collective-permute-start(bf16[2,128,1024]{2,1,0:T(8,128)(2,1)} %bitcast.13), channel_id=1, source_target_pairs={{0,32},{32,0},{1,33},{33,1},{2,34},{34,2},{3,35},{35,3},{4,36},{36... | collective-permute-start | bytes 1572872 | tf_op jit(solution)/shard_map/ppermute | solution.py:27
  41.0 12.1 %collective-permute-start.12 = (bf16[2,256,1024]{2,1,0:T(8,128)(2,1)S(1)}, bf16[2,256,1024]{2,1,0:T(8,128)(2,1)S(1)}, u32[]{:S(2)}, u32[]{:S(2)}) collective-permute-start(bf16[2,256,1024]{2,1,0:T(8,128)(2,1)S(1)} %maximum_select_fusion), channel_id=1, source_target_pairs={{0,1},{1,0},{2,3},{3,2},{4,5},{5,4},{6,7},{7,6},{8,9},{9,8},{10,11... | collective-permute-start | bytes 3145736 | tf_op jit(solution)/shard_map/ppermute | solution.py:27
  42.3 7.7 %collective-permute-start.10 = (bf16[64,1152]{1,0:T(8,128)(2,1)S(1)}, bf16[64,1152]{1,0:T(8,128)(2,1)S(1)}, u32[]{:S(2)}, u32[]{:S(2)}) collective-permute-start(bf16[64,1152]{1,0:T(8,128)(2,1)S(1)} %pad_maximum_fusion.7), channel_id=1, source_target_pairs={{0,16},{8,24},{16,0},{24,8},{1,17},{9,25},{17,1},{25,9},{2,18},{10... | collective-permute-start | bytes 442376 | tf_op jit(solution)/shard_map/ppermute | solution.py:27
  45.5 7.3 %collective-permute-start.9 = (bf16[64,1152]{1,0:T(8,128)(2,1)S(1)}, bf16[64,1152]{1,0:T(8,128)(2,1)S(1)}, u32[]{:S(2)}, u32[]{:S(2)}) collective-permute-start(bf16[64,1152]{1,0:T(8,128)(2,1)S(1)} %pad_maximum_fusion.7), channel_id=1, source_target_pairs={{0,8},{8,16},{16,24},{24,0},{1,9},{9,17},{17,25},{25,1},{2,10},{10... | collective-permute-start | bytes 442376 | tf_op jit(solution)/shard_map/ppermute | solution.py:27
  45.9 7.2 %collective-permute-start.11 = (bf16[64,1152]{1,0:T(8,128)(2,1)S(1)}, bf16[64,1152]{1,0:T(8,128)(2,1)S(1)}, u32[]{:S(2)}, u32[]{:S(2)}) collective-permute-start(bf16[64,1152]{1,0:T(8,128)(2,1)S(1)} %pad_maximum_fusion.7), channel_id=1, source_target_pairs={{0,24},{8,0},{16,8},{24,16},{1,25},{9,1},{17,9},{25,17},{2,26},{10... | collective-permute-start | bytes 442376 | tf_op jit(solution)/shard_map/ppermute | solution.py:27
  89.8 2.4 collective-permute-start.14
  92.5 10.1 %collective-permute-start.15 = (bf16[128,1024]{1,0:T(8,128)(2,1)S(1)}, bf16[128,1024]{1,0:T(8,128)(2,1)S(1)}, u32[]{:S(2)}, u32[]{:S(2)}) collective-permute-start(bf16[128,1024]{1,0:T(8,128)(2,1)S(1)} %fusion.24), channel_id=1, source_target_pairs={{0,32},{32,0},{1,33},{33,1},{2,34},{34,2},{3,35},{35,3},{4,36},{36... | collective-permute-start | bytes 786440 | tf_op jit(solution)/shard_map/ppermute | solution.py:27
  102.7 3.3 collective-permute-start.18
  106.0 23.2 %collective-permute-start.22 = (bf16[2,256,1024]{2,1,0:T(8,128)(2,1)}, bf16[2,256,1024]{2,1,0:T(8,128)(2,1)}, u32[]{:S(2)}, u32[]{:S(2)}) collective-permute-start(bf16[2,256,1024]{2,1,0:T(8,128)(2,1)} %maximum_select_fusion.1), channel_id=1, source_target_pairs={{0,1},{1,0},{2,3},{3,2},{4,5},{5,4},{6,7},{7,6},{8,9},{9,8},{10,11... | collective-permute-start | bytes 3145736 | tf_op jit(solution)/shard_map/ppermute | solution.py:27
  108.3 7.5 %collective-permute-start.19 = (bf16[128,1024]{1,0:T(8,128)(2,1)S(1)}, bf16[128,1024]{1,0:T(8,128)(2,1)S(1)}, u32[]{:S(2)}, u32[]{:S(2)}) collective-permute-start(bf16[128,1024]{1,0:T(8,128)(2,1)S(1)} %fusion.25), channel_id=1, source_target_pairs={{0,32},{32,0},{1,33},{33,1},{2,34},{34,2},{3,35},{35,3},{4,36},{36... | collective-permute-start | bytes 786440 | tf_op jit(solution)/shard_map/ppermute | solution.py:27
  108.6 8.5 %collective-permute-start.17 = (bf16[128,1024]{1,0:T(8,128)(2,1)S(1)}, bf16[128,1024]{1,0:T(8,128)(2,1)S(1)}, u32[]{:S(2)}, u32[]{:S(2)}) collective-permute-start(bf16[128,1024]{1,0:T(8,128)(2,1)S(1)} %fusion.19), channel_id=1, source_target_pairs={{0,96},{32,64},{64,32},{96,0},{1,97},{33,65},{65,33},{97,1},{2,98}... | collective-permute-start | bytes 786440 | tf_op jit(solution)/shard_map/ppermute | solution.py:756
  111.3 11.8 %collective-permute-start.16 = (bf16[128,1024]{1,0:T(8,128)(2,1)S(1)}, bf16[128,1024]{1,0:T(8,128)(2,1)}, u32[]{:S(2)}, u32[]{:S(2)}) collective-permute-start(bf16[128,1024]{1,0:T(8,128)(2,1)S(1)} %fusion.19), channel_id=1, source_target_pairs={{0,64},{32,96},{64,0},{96,32},{1,65},{33,97},{65,1},{97,33},{2,66}... | collective-permute-start | bytes 786440 | tf_op jit(solution)/shard_map/ppermute | solution.py:755
  125.5 8.4 %collective-permute-start.23 = (bf16[256,1024]{1,0:T(8,128)(2,1)S(1)}, bf16[256,1024]{1,0:T(8,128)(2,1)S(1)}, u32[]{:S(2)}, u32[]{:S(2)}) collective-permute-start(bf16[256,1024]{1,0:T(8,128)(2,1)S(1)} %get-tuple-element.256.refs_0_.refs_14_), channel_id=1, source_target_pairs={{0,1},{1,0},{2,3},{3,2},{4,5},{5,4},{6,7},{7,6},{8,9},{9,8},{10,11... | collective-permute-start | bytes 1572872 | tf_op jit(solution)/shard_map/ppermute | solution.py:27
  130.5 22.9 %collective-permute-start.21 = (bf16[128,1024]{1,0:T(8,128)(2,1)S(1)}, bf16[128,1024]{1,0:T(8,128)(2,1)S(1)}, u32[]{:S(2)}, u32[]{:S(2)}) collective-permute-start(bf16[128,1024]{1,0:T(8,128)(2,1)S(1)} %fusion.16), channel_id=1, source_target_pairs={{0,96},{32,64},{64,32},{96,0},{1,97},{33,65},{65,33},{97,1},{2,98}... | collective-permute-start | bytes 786440 | tf_op jit(solution)/shard_map/ppermute | solution.py:756
  133.7 19.8 %collective-permute-start.20 = (bf16[128,1024]{1,0:T(8,128)(2,1)S(1)}, bf16[128,1024]{1,0:T(8,128)(2,1)S(1)}, u32[]{:S(2)}, u32[]{:S(2)}) collective-permute-start(bf16[128,1024]{1,0:T(8,128)(2,1)S(1)} %fusion.16), channel_id=1, source_target_pairs={{0,64},{32,96},{64,0},{96,32},{1,65},{33,97},{65,1},{97,33},{2,66}... | collective-permute-start | bytes 786440 | tf_op jit(solution)/shard_map/ppermute | solution.py:755
  153.4 3.5 %collective-permute-start.24 = (bf16[256,1024]{1,0:T(8,128)(2,1)S(1)}, bf16[256,1024]{1,0:T(8,128)(2,1)S(1)}, u32[]{:S(2)}, u32[]{:S(2)}) collective-permute-start(bf16[256,1024]{1,0:T(8,128)(2,1)S(1)} %get-tuple-element.165), channel_id=1, source_target_pairs={{0,1},{1,0},{2,3},{3,2},{4,5},{5,4},{6,7},{7,6},{8,9},{9,8},{10,11... | collective-permute-start | bytes 1572872 | tf_op jit(solution)/shard_map/ppermute | solution.py:27
  155.4 2.5 collective-permute-start.26
  157.2 9.9 %collective-permute-start.25 = (bf16[128,1024]{1,0:T(8,128)(2,1)S(1)}, bf16[128,1024]{1,0:T(8,128)(2,1)S(1)}, u32[]{:S(2)}, u32[]{:S(2)}) collective-permute-start(bf16[128,1024]{1,0:T(8,128)(2,1)S(1)} %fusion.26), channel_id=1, source_target_pairs={{0,32},{32,0},{1,33},{33,1},{2,34},{34,2},{3,35},{35,3},{4,36},{36... | collective-permute-start | bytes 786440 | tf_op jit(solution)/shard_map/ppermute | solution.py:27
  167.2 14.5 %collective-permute-start.28 = (bf16[128,1024]{1,0:T(8,128)(2,1)S(1)}, bf16[128,1024]{1,0:T(8,128)(2,1)S(1)}, u32[]{:S(2)}, u32[]{:S(2)}) collective-permute-start(bf16[128,1024]{1,0:T(8,128)(2,1)S(1)} %fusion.13), channel_id=1, source_target_pairs={{0,96},{32,64},{64,32},{96,0},{1,97},{33,65},{65,33},{97,1},{2,98}... | collective-permute-start | bytes 786440 | tf_op jit(solution)/shard_map/ppermute | solution.py:756
  170.0 11.7 %collective-permute-start.27 = (bf16[128,1024]{1,0:T(8,128)(2,1)S(1)}, bf16[128,1024]{1,0:T(8,128)(2,1)S(1)}, u32[]{:S(2)}, u32[]{:S(2)}) collective-permute-start(bf16[128,1024]{1,0:T(8,128)(2,1)S(1)} %fusion.13), channel_id=1, source_target_pairs={{0,64},{32,96},{64,0},{96,32},{1,65},{33,97},{65,1},{97,33},{2,66}... | collective-permute-start | bytes 786440 | tf_op jit(solution)/shard_map/ppermute | solution.py:755
  183.1 4.0 %collective-permute-start.29 = (bf16[256,1024]{1,0:T(8,128)(2,1)}, bf16[256,1024]{1,0:T(8,128)(2,1)}, u32[]{:S(2)}, u32[]{:S(2)}) collective-permute-start(bf16[256,1024]{1,0:T(8,128)(2,1)} %get-tuple-element.181), channel_id=1, source_target_pairs={{0,1},{1,0},{2,3},{3,2},{4,5},{5,4},{6,7},{7,6},{8,9},{9,8},{10,11... | collective-permute-start | bytes 1572872 | tf_op jit(solution)/shard_map/ppermute | solution.py:27
  186.9 12.1 %collective-permute-start.33 = (bf16[256,1024]{1,0:T(8,128)(2,1)S(1)}, bf16[256,1024]{1,0:T(8,128)(2,1)S(1)}, u32[]{:S(2)}, u32[]{:S(2)}) collective-permute-start(bf16[256,1024]{1,0:T(8,128)(2,1)S(1)} %get-tuple-element.201.refs_0_.refs_2_.refs_6_), channel_id=1, source_target_pairs={{0,1},{1,0},{2,3},{3,2},{4,5},{5,4},{6,7},{7,6},{8,9},{9,8},{10,11... | collective-permute-start | bytes 1572872 | tf_op jit(solution)/shard_map/ppermute | solution.py:27
  188.6 7.2 %collective-permute-start.30 = (bf16[128,1024]{1,0:T(8,128)(2,1)S(1)}, bf16[128,1024]{1,0:T(8,128)(2,1)S(1)}, u32[]{:S(2)}, u32[]{:S(2)}) collective-permute-start(bf16[128,1024]{1,0:T(8,128)(2,1)S(1)} %fusion.27), channel_id=1, source_target_pairs={{0,32},{32,0},{1,33},{33,1},{2,34},{34,2},{3,35},{35,3},{4,36},{36... | collective-permute-start | bytes 786440 | tf_op jit(solution)/shard_map/ppermute | solution.py:27
  195.9 13.7 %collective-permute-start.32 = (bf16[128,1024]{1,0:T(8,128)(2,1)S(1)}, bf16[128,1024]{1,0:T(8,128)(2,1)S(1)}, u32[]{:S(2)}, u32[]{:S(2)}) collective-permute-start(bf16[128,1024]{1,0:T(8,128)(2,1)S(1)} %fusion.10), channel_id=1, source_target_pairs={{0,96},{32,64},{64,32},{96,0},{1,97},{33,65},{65,33},{97,1},{2,98}... | collective-permute-start | bytes 786440 | tf_op jit(solution)/shard_map/ppermute | solution.py:756
  198.7 11.0 %collective-permute-start.31 = (bf16[128,1024]{1,0:T(8,128)(2,1)S(1)}, bf16[128,1024]{1,0:T(8,128)(2,1)S(1)}, u32[]{:S(2)}, u32[]{:S(2)}) collective-permute-start(bf16[128,1024]{1,0:T(8,128)(2,1)S(1)} %fusion.10), channel_id=1, source_target_pairs={{0,64},{32,96},{64,0},{96,32},{1,65},{33,97},{65,1},{97,33},{2,66}... | collective-permute-start | bytes 786440 | tf_op jit(solution)/shard_map/ppermute | solution.py:755
  212.5 3.3 collective-permute-start.34
  217.2 23.0 %collective-permute-start.35 = (bf16[3,256,1024]{2,1,0:T(8,128)(2,1)}, bf16[3,256,1024]{2,1,0:T(8,128)(2,1)}, u32[]{:S(2)}, u32[]{:S(2)}) collective-permute-start(bf16[3,256,1024]{2,1,0:T(8,128)(2,1)} %pad_maximum_fusion), channel_id=1, source_target_pairs={{0,1},{1,0},{2,3},{3,2},{4,5},{5,4},{6,7},{7,6},{8,9},{9,8},{10,11... | collective-permute-start | bytes 4718600 | tf_op jit(solution)/shard_map/ppermute | solution.py:27
  234.7 2.8 collective-permute-start.40
  235.9 23.9 %collective-permute-start.43 = (bf16[256,1024]{1,0:T(8,128)(2,1)S(1)}, bf16[256,1024]{1,0:T(8,128)(2,1)S(1)}, u32[]{:S(2)}, u32[]{:S(2)}) collective-permute-start(bf16[256,1024]{1,0:T(8,128)(2,1)S(1)} %copy-done.109), channel_id=1, source_target_pairs={{0,1},{1,0},{2,3},{3,2},{4,5},{5,4},{6,7},{7,6},{8,9},{9,8},{10,11... | collective-permute-start | bytes 1572872 | tf_op jit(solution)/shard_map/ppermute | solution.py:27
  237.5 21.2 %collective-permute-start.41 = (f32[8,1024]{1,0:T(8,128)S(1)}, f32[8,1024]{1,0:T(8,128)S(1)}, u32[]{:S(2)}, u32[]{:S(2)}) collective-permute-start(f32[8,1024]{1,0:T(8,128)S(1)} %add.454), channel_id=1, source_target_pairs={{0,16},{8,24},{16,0},{24,8},{1,17},{9,25},{17,1},{25,9},{2,18},{10... | collective-permute-start | bytes 98312 | tf_op jit(solution)/shard_map/ppermute | solution.py:44
  244.0 23.3 %collective-permute-start.42 = (bf16[3,128,1024]{2,1,0:T(8,128)(2,1)S(1)}, bf16[3,128,1024]{2,1,0:T(8,128)(2,1)S(1)}, u32[]{:S(2)}, u32[]{:S(2)}) collective-permute-start(bf16[3,128,1024]{2,1,0:T(8,128)(2,1)S(1)} %fusion.6), channel_id=1, source_target_pairs={{0,32},{32,0},{1,33},{33,1},{2,34},{34,2},{3,35},{35,3},{4,36},{36... | collective-permute-start | bytes 2359304 | tf_op jit(solution)/shard_map/ppermute | solution.py:27
  256.9 7.3 %collective-permute-start.37 = (bf16[4,64,512]{2,0,1:T(4,128)(2,1)S(1)}, bf16[4,64,512]{2,0,1:T(4,128)(2,1)S(1)}, u32[]{:S(2)}, u32[]{:S(2)}) collective-permute-start(bf16[4,64,512]{2,0,1:T(4,128)(2,1)S(1)} %get-tuple-element.285), channel_id=1, source_target_pairs={{0,24},{8,0},{16,8},{24,16},{1,25},{9,1},{17,9},{25,17},{2,26},{10... | collective-permute-start | bytes 786440 | tf_op jit(solution)/shard_map/ppermute | solution.py:27
  257.9 8.6 %collective-permute-start.36 = (bf16[4,64,512]{2,0,1:T(4,128)(2,1)S(1)}, bf16[4,64,512]{2,0,1:T(4,128)(2,1)S(1)}, u32[]{:S(2)}, u32[]{:S(2)}) collective-permute-start(bf16[4,64,512]{2,0,1:T(4,128)(2,1)S(1)} %get-tuple-element.286), channel_id=1, source_target_pairs={{0,8},{8,16},{16,24},{24,0},{1,9},{9,17},{17,25},{25,1},{2,10},{10... | collective-permute-start | bytes 786440 | tf_op jit(solution)/shard_map/ppermute | solution.py:27
  258.7 7.8 %collective-permute-start.39 = (bf16[4,64,512]{2,1,0:T(8,128)(2,1)S(1)}, bf16[4,64,512]{2,1,0:T(8,128)(2,1)S(1)}, u32[]{:S(2)}, u32[]{:S(2)}) collective-permute-start(bf16[4,64,512]{2,1,0:T(8,128)(2,1)S(1)} %get-tuple-element.283), channel_id=1, source_target_pairs={{0,6},{2,0},{4,2},{6,4},{1,7},{3,1},{5,3},{7,5},{8,14},{10,8},{12,... | collective-permute-start | bytes 786440 | tf_op jit(solution)/shard_map/ppermute | solution.py:27
  259.8 7.6 %collective-permute-start.38 = (bf16[4,64,512]{2,1,0:T(8,128)(2,1)S(1)}, bf16[4,64,512]{2,1,0:T(8,128)(2,1)S(1)}, u32[]{:S(2)}, u32[]{:S(2)}) collective-permute-start(bf16[4,64,512]{2,1,0:T(8,128)(2,1)S(1)} %get-tuple-element.284), channel_id=1, source_target_pairs={{0,2},{2,4},{4,6},{6,0},{1,3},{3,5},{5,7},{7,1},{8,10},{10,12},{12... | collective-permute-start | bytes 786440 | tf_op jit(solution)/shard_map/ppermute | solution.py:27
  267.4 7.2 %collective-permute-start.48 = (f32[8,1024]{1,0:T(8,128)S(1)}, f32[8,1024]{1,0:T(8,128)S(1)}, u32[]{:S(2)}, u32[]{:S(2)}) collective-permute-start(f32[8,1024]{1,0:T(8,128)S(1)} %add.467), channel_id=1, source_target_pairs={{0,2},{2,0},{4,6},{6,4},{1,3},{3,1},{5,7},{7,5},{8,10},{10,8},{12,... | collective-permute-start | bytes 98312 | tf_op jit(solution)/shard_map/ppermute | solution.py:44
  268.0 13.9 %collective-permute-start.44 = (bf16[4,64,1024]{2,0,1:T(4,128)(2,1)S(1)}, bf16[4,64,1024]{2,0,1:T(4,128)(2,1)S(1)}, u32[]{:S(2)}, u32[]{:S(2)}) collective-permute-start(bf16[4,64,1024]{2,0,1:T(4,128)(2,1)S(1)} %pad_maximum_fusion.1), channel_id=1, source_target_pairs={{0,8},{8,16},{16,24},{24,0},{1,9},{9,17},{17,25},{25,1},{2,10},{10... | collective-permute-start | bytes 1572872 | tf_op jit(solution)/shard_map/ppermute | solution.py:27
  268.8 13.1 %collective-permute-start.45 = (bf16[4,64,1024]{2,0,1:T(4,128)(2,1)S(1)}, bf16[4,64,1024]{2,0,1:T(4,128)(2,1)S(1)}, u32[]{:S(2)}, u32[]{:S(2)}) collective-permute-start(bf16[4,64,1024]{2,0,1:T(4,128)(2,1)S(1)} %pad_maximum_fusion.2), channel_id=1, source_target_pairs={{0,24},{8,0},{16,8},{24,16},{1,25},{9,1},{17,9},{25,17},{2,26},{10... | collective-permute-start | bytes 1572872 | tf_op jit(solution)/shard_map/ppermute | solution.py:27
  271.3 13.3 %collective-permute-start.46 = (bf16[4,64,1024]{2,1,0:T(8,128)(2,1)S(1)}, bf16[4,64,1024]{2,1,0:T(8,128)(2,1)S(1)}, u32[]{:S(2)}, u32[]{:S(2)}) collective-permute-start(bf16[4,64,1024]{2,1,0:T(8,128)(2,1)S(1)} %pad_maximum_fusion.3), channel_id=1, source_target_pairs={{0,2},{2,4},{4,6},{6,0},{1,3},{3,5},{5,7},{7,1},{8,10},{10,12},{12... | collective-permute-start | bytes 1572872 | tf_op jit(solution)/shard_map/ppermute | solution.py:27
  272.9 11.7 %collective-permute-start.47 = (bf16[4,64,1024]{2,1,0:T(8,128)(2,1)S(1)}, bf16[4,64,1024]{2,1,0:T(8,128)(2,1)S(1)}, u32[]{:S(2)}, u32[]{:S(2)}) collective-permute-start(bf16[4,64,1024]{2,1,0:T(8,128)(2,1)S(1)} %pad_maximum_fusion.4), channel_id=1, source_target_pairs={{0,6},{2,0},{4,2},{6,4},{1,7},{3,1},{5,3},{7,5},{8,14},{10,8},{12,... | collective-permute-start | bytes 1572872 | tf_op jit(solution)/shard_map/ppermute | solution.py:27
  274.5 5.9 %collective-permute-start.49 = (bf16[128,1024]{1,0:T(8,128)(2,1)S(1)}, bf16[128,1024]{1,0:T(8,128)(2,1)S(1)}, u32[]{:S(2)}, u32[]{:S(2)}) collective-permute-start(bf16[128,1024]{1,0:T(8,128)(2,1)S(1)} %fusion.28), channel_id=1, source_target_pairs={{0,32},{32,0},{1,33},{33,1},{2,34},{34,2},{3,35},{35,3},{4,36},{36... | collective-permute-start | bytes 786440 | tf_op jit(solution)/shard_map/ppermute | solution.py:27
  285.5 8.0 %collective-permute-start.56 = (f32[8,1024]{1,0:T(8,128)S(1)}, f32[8,1024]{1,0:T(8,128)S(1)}, u32[]{:S(2)}, u32[]{:S(2)}) collective-permute-start(f32[8,1024]{1,0:T(8,128)S(1)} %add.482), channel_id=1, source_target_pairs={{0,4},{2,6},{4,0},{6,2},{1,5},{3,7},{5,1},{7,3},{8,12},{10,14},{12... | collective-permute-start | bytes 98312 | tf_op jit(solution)/shard_map/ppermute | solution.py:44
  287.9 5.9 %collective-permute-start.55 = (bf16[64,1024]{1,0:T(8,128)(2,1)S(1)}, bf16[64,1024]{1,0:T(8,128)(2,1)}, u32[]{:S(2)}, u32[]{:S(2)}) collective-permute-start(bf16[64,1024]{1,0:T(8,128)(2,1)S(1)} %get-tuple-element.280), channel_id=1, source_target_pairs={{0,16},{8,24},{16,0},{24,8},{1,17},{9,25},{17,1},{25,9},{2,18},{10... | collective-permute-start | bytes 393224 | tf_op jit(solution)/shard_map/ppermute | solution.py:27
  289.6 7.1 %collective-permute-start.54 = (bf16[64,1024]{1,0:T(8,128)(2,1)S(1)}, bf16[64,1024]{1,0:T(8,128)(2,1)}, u32[]{:S(2)}, u32[]{:S(2)}) collective-permute-start(bf16[64,1024]{1,0:T(8,128)(2,1)S(1)} %get-tuple-element.281), channel_id=1, source_target_pairs={{0,24},{8,0},{16,8},{24,16},{1,25},{9,1},{17,9},{25,17},{2,26},{10... | collective-permute-start | bytes 393224 | tf_op jit(solution)/shard_map/ppermute | solution.py:27
  290.0 23.6 %collective-permute-start.53 = (bf16[64,1024]{1,0:T(8,128)(2,1)}, bf16[64,1024]{1,0:T(8,128)(2,1)}, u32[]{:S(2)}, u32[]{:S(2)}) collective-permute-start(bf16[64,1024]{1,0:T(8,128)(2,1)} %get-tuple-element.282), channel_id=1, source_target_pairs={{0,8},{8,16},{16,24},{24,0},{1,9},{9,17},{17,25},{25,1},{2,10},{10... | collective-permute-start | bytes 393224 | tf_op jit(solution)/shard_map/ppermute | solution.py:27
  292.0 21.6 %collective-permute-start.52 = (bf16[64,1792]{1,0:T(8,128)(2,1)}, bf16[64,1792]{1,0:T(8,128)(2,1)}, u32[]{:S(2)}, u32[]{:S(2)}) collective-permute-start(bf16[64,1792]{1,0:T(8,128)(2,1)} %get-tuple-element.277), channel_id=1, source_target_pairs={{0,4},{2,6},{4,0},{6,2},{1,5},{3,7},{5,1},{7,3},{8,12},{10,14},{12... | collective-permute-start | bytes 688136 | tf_op jit(solution)/shard_map/ppermute | solution.py:27
  293.5 20.1 %collective-permute-start.50 = (bf16[64,1792]{1,0:T(8,128)(2,1)}, bf16[64,1792]{1,0:T(8,128)(2,1)}, u32[]{:S(2)}, u32[]{:S(2)}) collective-permute-start(bf16[64,1792]{1,0:T(8,128)(2,1)} %get-tuple-element.278), channel_id=1, source_target_pairs={{0,2},{2,4},{4,6},{6,0},{1,3},{3,5},{5,7},{7,1},{8,10},{10,12},{12... | collective-permute-start | bytes 688136 | tf_op jit(solution)/shard_map/ppermute | solution.py:27
  294.1 19.5 %collective-permute-start.51 = (bf16[64,1792]{1,0:T(8,128)(2,1)}, bf16[64,1792]{1,0:T(8,128)(2,1)}, u32[]{:S(2)}, u32[]{:S(2)}) collective-permute-start(bf16[64,1792]{1,0:T(8,128)(2,1)} %get-tuple-element.279), channel_id=1, source_target_pairs={{0,6},{2,0},{4,2},{6,4},{1,7},{3,1},{5,3},{7,5},{8,14},{10,8},{12,... | collective-permute-start | bytes 688136 | tf_op jit(solution)/shard_map/ppermute | solution.py:27
  310.4 4.0 %collective-permute-start.57 = (bf16[64,1024]{1,0:T(8,128)(2,1)}, bf16[64,1024]{1,0:T(8,128)(2,1)S(1)}, u32[]{:S(2)}, u32[]{:S(2)}) collective-permute-start(bf16[64,1024]{1,0:T(8,128)(2,1)} %reduce-scatter.2.cloned.1.call-done), channel_id=1, source_target_pairs={{0,32},{32,0},{1,33},{33,1},{2,34},{34,2},{3,35},{35,3},{4,36},{36... | collective-permute-start | bytes 393224 | tf_op jit(solution)/shard_map/ppermute | solution.py:27
  315.7 3.7 %collective-permute-start.59 = (f32[8,1024]{1,0:T(8,128)S(1)}, f32[8,1024]{1,0:T(8,128)S(1)}, u32[]{:S(2)}, u32[]{:S(2)}) collective-permute-start(f32[8,1024]{1,0:T(8,128)S(1)} %add.490), channel_id=1, source_target_pairs={{0,1},{1,0},{2,3},{3,2},{4,5},{5,4},{6,7},{7,6},{8,9},{9,8},{10,11... | collective-permute-start | bytes 98312 | tf_op jit(solution)/shard_map/ppermute | solution.py:27
  320.8 3.6 %collective-permute-start.61 = (bf16[32,1024]{1,0:T(8,128)(2,1)S(1)}, bf16[32,1024]{1,0:T(8,128)(2,1)S(1)}, u32[]{:S(2)}, u32[]{:S(2)}) collective-permute-start(bf16[32,1024]{1,0:T(8,128)(2,1)S(1)} %add_convert_fusion.4.out_own), channel_id=1, source_target_pairs={{0,32},{32,0},{1,33},{33,1},{2,34},{34,2},{3,35},{35,3},{4,36},{36... | collective-permute-start | bytes 196616 | tf_op jit(solution)/shard_map/ppermute | solution.py:27
  322.2 3.3 collective-permute-start.62
  322.5 8.0 %collective-permute-start.60 = (bf16[64,1792]{1,0:T(8,128)(2,1)S(1)}, bf16[64,1792]{1,0:T(8,128)(2,1)S(1)}, u32[]{:S(2)}, u32[]{:S(2)}) collective-permute-start(bf16[64,1792]{1,0:T(8,128)(2,1)S(1)} %maximum_select_fusion.10), channel_id=1, source_target_pairs={{0,32},{32,0},{1,33},{33,1},{2,34},{34,2},{3,35},{35,3},{4,36},{36... | collective-permute-start | bytes 688136 | tf_op jit(solution)/shard_map/ppermute | solution.py:27
  (114 other events, 1262.1 us)
Sparse Core Ops, SparseCore 0:
  13.5 64.9 all-gather.1
  236.0 74.3 reduce-scatter.1
where the time goes:
time: 346 us; the launch traced here: 339 us
  waiting for transfers between devices  97.3 us (28%)
  Pallas kernels  75.2 us (22%)
  starting transfers between devices  72.1 us (21%)
  local copies, waits for them, and re-layouts  43.3 us (13%)
  other arithmetic  35 us (10%)
  between operations  16.3 us (5%)
    ppermute x51, starting transfers between devices, shift(): lax.ppermute(block, axis, [(i, (i + distance) % size) for i in range(size)])  54.1 us
    ppermute x51, waiting for transfers between devices, shift(): lax.ppermute(block, axis, [(i, (i + distance) % size) for i in range(size)])  52.1 us
    pallas_call x8, Pallas kernels, call(): pl.pallas_call(body, in_specs=[pl.BlockSpec(memory_space=pltpu.VMEM)] * l...  51.1 us
    unnamed x227, local copies, waits for them, and re-layouts  27 us
    pallas_call x2, Pallas kernels, own_call(): pl.pallas_call(body, in_specs=[pl.BlockSpec(memory_space=pltpu.HBM)] * le...  21.9 us
    all_gather x1, waiting for transfers between devices, fetch_layer(): weights = lax.all_gather(block, ('y', 'x'), axis=0, tiled=True)  21.8 us
    reduce_scatter x1, waiting for transfers between devices, shards(): lax.psum_scatter(down, ('y', 'x'), scatter_dimension=0, tiled=True)  13.7 us
    ppermute x4, starting transfers between devices, send_on(): lax.ppermute(block, ('section', 'ctx'), [(i, 3 - i) for i in range(4)])  11.4 us
  transfers between devices with their start and end apart: 65, of which 29 were waited for; matrix products, arithmetic and copies ran while one was open for 13% of the time, Pallas kernels for 20%

commit v1 on v0

--- a/solution.py
+++ b/solution.py
@@ -689,10 +689,8 @@
         jnp.arange(4)[:, None, None] == 2 * c + k, out, jnp.zeros_like(out)
     )
     one = jnp.concatenate([one[:, :, : SPLIT], out], -1)
-    ones, twos, (more, down_more) = together(
-        direct(one, "x", 0),
-        direct(two, "y", 0),
-        [shift_pair(sums, "x", 2), shift(down, "ctx", 1)],
+    ones, twos, (more,) = together(
+        direct(one, "x", 0), direct(two, "y", 0), [shift_pair(sums, "x", 2)]
     )
     sums = sums + more
     one = plus(quarter_of(one, 0, x), *ones)
@@ -707,8 +705,8 @@
     sums = in_order(k, sums[None], more[None], 0)
     block = in_order(k, mine[:, :width], other[:, :width], 0)
     out = plus(mine[:, width:], other[:, width:])
-    (block_more, out_more, sums_more), _ = together(
-        [shift(block, "ctx", 1), shift(out, "ctx", 1), shift(sums, "ctx", 1)], [beside]
+    (block_more, out_more, sums_more, down_more), _ = together(
+        [shift(item, "ctx", 1) for item in (block, out, sums, down)], [beside]
     )
     place = (4 * y + x) * 2 + k
     vectors = [((1, width), FULL) for width in SMALL]

time: 346 us -> 366 us (1.058)
  the two profiles are of different devices: /device:TPU:1 before, /device:TPU:0 now
where the time goes in v1:
time: 366 us; the launch traced here: 359 us
  waiting for transfers between devices  113 us (31%)
  Pallas kernels  75.2 us (21%)
  starting transfers between devices  70.1 us (19%)
  local copies, waits for them, and re-layouts  46.9 us (13%)
  other arithmetic  37 us (10%)
  between operations  16.3 us (4%)
    ppermute x51, waiting for transfers between devices, shift(): lax.ppermute(block, axis, [(i, (i + distance) % size) for i in range(size)])  56.2 us
    pallas_call x8, Pallas kernels, call(): pl.pallas_call(body, in_specs=[pl.BlockSpec(memory_space=pltpu.VMEM)] * l...  51.1 us
    ppermute x51, starting transfers between devices, shift(): lax.ppermute(block, axis, [(i, (i + distance) % size) for i in range(size)])  50.9 us
    unnamed x223, local copies, waits for them, and re-layouts  26.6 us
    reduce_scatter x1, waiting for transfers between devices, shards(): lax.psum_scatter(down, ('y', 'x'), scatter_dimension=0, tiled=True)  25.7 us
    pallas_call x2, Pallas kernels, own_call(): pl.pallas_call(body, in_specs=[pl.BlockSpec(memory_space=pltpu.HBM)] * le...  22 us
    all_gather x1, waiting for transfers between devices, fetch_layer(): weights = lax.all_gather(block, ('y', 'x'), axis=0, tiled=True)  20.8 us
    ppermute x4, starting transfers between devices, send_on(): lax.ppermute(block, ('section', 'ctx'), [(i, 3 - i) for i in range(4)])  12.6 us
  transfers between devices with their start and end apart: 65, of which 32 were waited for; matrix products, arithmetic and copies ran while one was open for 14% of the time, Pallas kernels for 18%

profile of v1, /device:TPU:0, one launch (start us, length us, event | category | flops | bytes accessed | tf_op | source)
XLA Modules:
  0.0 358.8 jit_solution(12498199744204852388)
XLA Ops:
  12.8 2.1 collective-permute-start.1
  17.6 2.1 collective-permute-start.8
  19.7 1.9 fusion.7
  23.5 2.8 collective-permute-start.7
  28.1 5.8 %collective-permute-done.7 = bf16[64,1152]{1,0:T(8,128)(2,1)S(1)} collective-permute-done((bf16[64,1152]{1,0:T(8,128)(2,1)S(1)}, bf16[64,1152]{1,0:T(8,128)(2,1)S(1)}, u32[]{:S(2)}, u32[]{:S(2)}) %collective-permute-start.7) | collective-permute-done | bytes 147488 | tf_op jit(solution)/shard_map/ppermute | solution.py:27
  33.9 2.6 collective-permute-done.6
  36.5 3.7 %collective-permute-done.5 = bf16[64,1152]{1,0:T(8,128)(2,1)S(1)} collective-permute-done((bf16[64,1152]{1,0:T(8,128)(2,1)S(1)}, bf16[64,1152]{1,0:T(8,128)(2,1)S(1)}, u32[]{:S(2)}, u32[]{:S(2)}) %collective-permute-start.5) | collective-permute-done | bytes 147488 | tf_op jit(solution)/shard_map/ppermute | solution.py:27
  41.0 3.4 collective-permute-start.10
  45.1 3.0 collective-permute-start.11
  49.5 3.0 collective-permute-done.9
  56.9 20.8 %all-gather.2.cloned.1.call-done.refs_7_.refs_12_.refs_13_.refs_15_ = bf16[1024,2816]{1,0:T(8,128)(2,1)} async-done(((bf16[64,2816]{1,0:T(8,128)(2,1)}), bf16[1024,2816]{1,0:T(8,128)(2,1)}) %all-gather.2.cloned.1.call-update) | async-done | bytes 5767184 | tf_op jit(solution)/shard_map/all_gather | solution.py:621
  79.6 2.6 copy-done.46
  82.3 6.8 %layer_forward.4 = (bf16[256,1024]{1,0:T(8,128)(2,1)S(1)}, bf16[256,1024]{1,0:T(8,128)(2,1)}) custom-call(bf16[256,1024]{1,0:T(8,128)(2,1)S(1)} %get-tuple-element.270.refs_0_, bf16[256,1024]{1,0:T(8,128)(2,1)S(1)} %get-tuple-element.276.refs_1_, s32[2,1,256]{2,1,0:T(1,128)S(1)} %get-tuple-element.310.refs_2_.refs_3_, ...), custom_call_target="tpu_custom_call" | custom-call | flops 8589934592 | bytes 8388608 | tf_op jit(solution)/shard_map/layer_forward/pallas_call | solution.py:332
  91.4 1.8 collective-permute-start.15
  93.2 2.6 copy-done.47
  95.9 5.9 %layer_forward.5 = (bf16[256,1024]{1,0:T(8,128)(2,1)S(1)}, bf16[256,1024]{1,0:T(8,128)(2,1)S(1)}) custom-call(bf16[256,1024]{1,0:T(8,128)(2,1)S(1)} %get-tuple-element.150.refs_0_, bf16[256,1024]{1,0:T(8,128)(2,1)S(1)} %get-tuple-element.275.refs_1_, s32[2,1,256]{2,1,0:T(1,128)S(1)} %get-tuple-element.309.refs_2_.refs_3_, ...), custom_call_target="tpu_custom_call" | custom-call | flops 8589934592 | bytes 8388608 | tf_op jit(solution)/shard_map/layer_forward/pallas_call | solution.py:332
  102.0 2.6 maximum_select_fusion.1
  107.9 2.9 collective-permute-start.17
  111.5 5.1 %collective-permute-done.19 = bf16[128,1024]{1,0:T(8,128)(2,1)S(1)} collective-permute-done((bf16[128,1024]{1,0:T(8,128)(2,1)S(1)}, bf16[128,1024]{1,0:T(8,128)(2,1)S(1)}, u32[]{:S(2)}, u32[]{:S(2)}) %collective-permute-start.19) | collective-permute-done | bytes 262176 | tf_op jit(solution)/shard_map/ppermute | solution.py:27
  117.9 4.1 %collective-permute-done.17 = bf16[128,1024]{1,0:T(8,128)(2,1)S(1)} collective-permute-done((bf16[128,1024]{1,0:T(8,128)(2,1)S(1)}, bf16[128,1024]{1,0:T(8,128)(2,1)S(1)}, u32[]{:S(2)}, u32[]{:S(2)}) %collective-permute-start.17) | collective-permute-done | bytes 262176 | tf_op jit(solution)/shard_map/ppermute | solution.py:754
  123.0 2.4 broadcast_select_fusion.4
  125.4 2.5 fusion.51
  129.1 3.4 collective-permute-start.21
  132.8 2.6 copy-done.48
  135.4 6.2 %layer_forward.6 = (bf16[256,1024]{1,0:T(8,128)(2,1)S(1)}, bf16[256,1024]{1,0:T(8,128)(2,1)S(1)}, bf16[512,1024]{1,0:T(8,128)(2,1)S(1)}, bf16[512,1024]{1,0:T(8,...) custom-call(bf16[256,1024]{1,0:T(8,128)(2,1)S(1)} %get-tuple-element, ...), custom_call_target="tpu_custom_call" | custom-call | flops 8589934592 | bytes 8388608 | tf_op jit(solution)/shard_map/layer_forward/pallas_call | solution.py:332
  145.3 7.0 %layer_backward.3 = (bf16[256,1024]{1,0:T(8,128)(2,1)S(1)}, bf16[256,1024]{1,0:T(8,128)(2,1)S(1)}) custom-call(bf16[256,1024]{1,0:T(8,128)(2,1)S(1)} %get-tuple-element.266.refs_0_, bf16[256,1024]{1,0:T(8,128)(2,1)S(1)} %get-tuple-element.274.refs_1_, bf16[256,1152]{1,0:T(8,128)(2,1)S(1)} %bitcast.240, s32[2,1,256]{2,1,0:T(1,128)S(1)} %get-tuple-element.310.refs_2_.refs_3_, ...), custom_call_target="tpu_custom_call" | custom-call | flops 8589934592 | bytes 8388608 | tf_op jit(solution)/shard_map/layer_backward/pallas_call | solution.py:332
  157.0 6.3 %layer_forward.7 = (bf16[256,1024]{1,0:T(8,128)(2,1)S(1)}, bf16[256,1024]{1,0:T(8,128)(2,1)S(1)}, bf16[512,1024]{1,0:T(8,128)(2,1)S(1)}, bf16[512,1024]{1,0:T(8,...) custom-call(bf16[256,1024]{1,0:T(8,128)(2,1)S(1)} %get-tuple-element, ...), custom_call_target="tpu_custom_call" | custom-call | flops 8589934592 | bytes 8388608 | tf_op jit(solution)/shard_map/layer_forward/pallas_call | solution.py:332
  166.2 3.2 collective-permute-start.28
  169.6 7.9 %layer_backward.4 = (bf16[256,1024]{1,0:T(8,128)(2,1)S(1)}, bf16[256,1024]{1,0:T(8,128)(2,1)}) custom-call(bf16[256,1024]{1,0:T(8,128)(2,1)S(1)} %get-tuple-element.169.refs_0_, bf16[256,1024]{1,0:T(8,128)(2,1)S(1)} %get-tuple-element.273.refs_1_, bf16[256,1152]{1,0:T(8,128)(2,1)S(1)} %bitcast.242, s32[2,1,256]{2,1,0:T(1,128)S(1)} %get-tuple-element.309.refs_2_.refs_3_, ...), custom_call_target="tpu_custom_call" | custom-call | flops 8589934592 | bytes 8388608 | tf_op jit(solution)/shard_map/layer_backward/pallas_call | solution.py:332
  178.4 3.1 collective-permute-done.28
  182.9 2.6 broadcast_select_fusion.2
  186.1 1.7 convert_add_fusion.4
  188.0 8.0 %collective-permute-done.30 = bf16[128,1024]{1,0:T(8,128)(2,1)S(1)} collective-permute-done((bf16[128,1024]{1,0:T(8,128)(2,1)S(1)}, bf16[128,1024]{1,0:T(8,128)(2,1)S(1)}, u32[]{:S(2)}, u32[]{:S(2)}) %collective-permute-start.30) | collective-permute-done | bytes 262176 | tf_op jit(solution)/shard_map/ppermute | solution.py:27
  196.1 3.0 collective-permute-start.32
  199.4 2.6 copy-done.49
  202.1 7.4 %layer_backward.5 = (bf16[256,1024]{1,0:T(8,128)(2,1)S(1)}, bf16[256,1024]{1,0:T(8,128)(2,1)S(1)}, bf16[512,1024]{1,0:T(8,128)(2,1)S(1)}, bf16[512,768]{1,0:T(8,128)(2,1)S(1)}, f32[8,1024]{1,0:T(8,128)S(1)}) custom-call(bf16[256,1024]{1,0:T(8,128)(2,1)S(1)} %get-tuple-element.201.refs_0_.refs_2_.refs_6_, ...), custom_call_target="tpu_custom_call" | custom-call | flops 8589934592 | bytes 8388608 | tf_op jit(solution)/shard_map/layer_backward/pallas_call | solution.py:332
  210.1 2.7 broadcast_select_fusion.1
  212.8 1.9 collective-permute-done.34.refs_5_.refs_1_.refs_9_
  216.7 3.7 %down_gradient.1 = bf16[1024,1024]{1,0:T(8,128)(2,1)} custom-call(bf16[512,1024]{1,0:T(8,128)(2,1)S(1)} %get-tuple-element.195.refs_0_, bf16[512,1024]{1,0:T(8,128)(2,1)S(1)} %copy-done.12, bf16[256,1024]{1,0:T(8,128)(2,1)S(1)} %get-tuple-element.201.refs_0_.refs_2_.refs_6_, bf16[256,1024]{1,0:T(8,128)(2,1)S(1)} %collective-permute-done.33.refs_1_.refs_3_.refs_7_, ...), custom_call_target="tpu_custom_call" | custom-call | tf_op jit(solution)/shard_map/down_gradient/pallas_call | solution.py:332
  220.4 12.2 %layer_backward_alone.1 = (bf16[256,1024]{1,0:T(8,128)(2,1)}, bf16[256,1024]{1,0:T(8,128)(2,1)}, bf16[512,1024]{1,0:T(8,128)(2,1)}, bf16[512,768]{1,0:T(8,128)(2,1)}, f32[8,1024]{1,0:T(8,128)}) custom-call(bf16[256,1024]{1,0:T(8,128)(2,1)} %copy-done.3, bf16[256,1024]{1,0:T(8,128)(2,1)} %copy-done.5, bf16[256,1152]{1,0:T(8,128)(2,1)} %bitcast.243, ...), custom_call_target="tpu_custom_call" | custom-call | flops 8589934592 | bytes 8388608 | tf_op jit(solution)/shard_map/layer_backward_alone/pallas_call | solution.py:413
  233.4 1.4 collective-permute-start.40
  234.9 2.4 collective-permute-done.40
  237.3 2.9 collective-permute-start.41
  240.3 2.0 convert_add_fusion
  242.3 1.7 copy-done.68
  245.7 9.8 %weight_gradients.1 = (bf16[1024,1024]{1,0:T(8,128)(2,1)}, bf16[1024,1024]{1,0:T(8,128)(2,1)}) custom-call(bf16[512,1024]{1,0:T(8,128)(2,1)} %copy-done.7, bf16[512,1024]{1,0:T(8,128)(2,1)} %copy-done.9, bf16[512,1024]{1,0:T(8,128)(2,1)} %copy-done.10, bf16[512,1024]{1,0:T(8,128)(2,1)} %get-tuple-element.198.refs_3_, bf16[512,256]{1,0:T(8,128)(2,1)} %copy-done.29, ...), custom_call_target="tpu_custom_call" | custom-call | tf_op jit(solution)/shard_map/weight_gradients/pallas_call | solution.py:413
  255.6 2.8 constant_dynamic-slice_fusion
  265.1 1.4 copy.76
  267.3 1.7 collective-permute-done.36
  269.4 2.4 collective-permute-done.38
  276.1 3.1 collective-permute-start.45
  279.2 2.1 collective-permute-start.46
  282.9 1.7 collective-permute-start.49
  284.6 1.6 fusion.1
  287.2 2.4 collective-permute-done.49
  290.0 3.2 collective-permute-done.46
  297.3 1.7 collective-permute-start.55
  301.2 2.3 collective-permute-start.52
  304.1 2.6 collective-permute-start.51
  307.8 1.8 collective-permute-done.52
  309.6 3.1 collective-permute-done.50
  318.3 25.7 %reduce-scatter.2.cloned.1.call-done = bf16[64,1024]{1,0:T(8,128)(2,1)} async-done(((bf16[1024,1024]{1,0:T(8,128)(2,1)}), bf16[64,1024]{1,0:T(8,128)(2,1)}) %reduce-scatter.2.cloned.1.call-update) | async-done | bytes 131088 | tf_op jit(solution)/shard_map/reduce_scatter | solution.py:874
  344.0 1.6 collective-permute-start.62
  345.6 3.5 collective-permute-done.62
  (447 shorter events, 81.6 us)
Async XLA Ops:
  7.3 70.4 %all-gather.2.cloned.1.call-start = ((), (), s32[]{:S(2)}) async-start(), calls=%async_computation.1 | async-start | bytes 6127616 | tf_op jit(solution)/shard_map/all_gather | solution.py:621
  10.1 1.4 collective-permute-start
  12.3 331.6 %reduce-scatter.2.cloned.1.call-start = ((), (), s32[]{:S(2)}) async-start(), calls=%async_computation.2 | async-start | bytes 2228224 | tf_op jit(solution)/shard_map/reduce_scatter | solution.py:874
  12.8 3.6 %collective-permute-start.1 = (s32[2,128]{1,0:T(2,128)S(1)}, s32[2,128]{1,0:T(2,128)S(1)}, u32[]{:S(2)}, u32[]{:S(2)}) collective-permute-start(s32[2,128]{1,0:T(2,128)S(1)} %bitcast.323), channel_id=1, source_target_pairs={{0,32},{32,0},{1,33},{33,1},{2,34},{34,2},{3,35},{35,3},{4,36},{36... | collective-permute-start | bytes 3080 | tf_op jit(solution)/shard_map/ppermute | solution.py:27
  14.8 1.6 collective-permute-start.3
  14.8 8.6 %collective-permute-start.4 = (bf16[32,1152]{1,0:T(8,128)(2,1)S(1)}, bf16[32,1152]{1,0:T(8,128)(2,1)S(1)}, u32[]{:S(2)}, u32[]{:S(2)}) collective-permute-start(bf16[32,1152]{1,0:T(8,128)(2,1)S(1)} %fusion.45), channel_id=1, source_target_pairs={{0,1},{1,0},{2,3},{3,2},{4,5},{5,4},{6,7},{7,6},{8,9},{9,8},{10,11... | collective-permute-start | bytes 221192 | tf_op jit(solution)/shard_map/ppermute | solution.py:27
  17.6 22.6 %collective-permute-start.8 = (bf16[2,128,1024]{2,1,0:T(8,128)(2,1)S(1)}, bf16[2,128,1024]{2,1,0:T(8,128)(2,1)S(1)}, u32[]{:S(2)}, u32[]{:S(2)}) collective-permute-start(bf16[2,128,1024]{2,1,0:T(8,128)(2,1)S(1)} %bitcast.281), channel_id=1, source_target_pairs={{0,32},{32,0},{1,33},{33,1},{2,34},{34,2},{3,35},{35,3},{4,36},{36... | collective-permute-start | bytes 1572872 | tf_op jit(solution)/shard_map/ppermute | solution.py:27
  23.5 10.4 %collective-permute-start.7 = (bf16[64,1152]{1,0:T(8,128)(2,1)S(1)}, bf16[64,1152]{1,0:T(8,128)(2,1)S(1)}, u32[]{:S(2)}, u32[]{:S(2)}) collective-permute-start(bf16[64,1152]{1,0:T(8,128)(2,1)S(1)} %maximum_select_fusion.11), channel_id=1, source_target_pairs={{0,6},{2,0},{4,2},{6,4},{1,7},{3,1},{5,3},{7,5},{8,14},{10,8},{12,... | collective-permute-start | bytes 442376 | tf_op jit(solution)/shard_map/ppermute | solution.py:27
  26.3 10.1 %collective-permute-start.6 = (bf16[64,1152]{1,0:T(8,128)(2,1)S(1)}, bf16[64,1152]{1,0:T(8,128)(2,1)S(1)}, u32[]{:S(2)}, u32[]{:S(2)}) collective-permute-start(bf16[64,1152]{1,0:T(8,128)(2,1)S(1)} %maximum_select_fusion.11), channel_id=1, source_target_pairs={{0,4},{2,6},{4,0},{6,2},{1,5},{3,7},{5,1},{7,3},{8,12},{10,14},{12... | collective-permute-start | bytes 442376 | tf_op jit(solution)/shard_map/ppermute | solution.py:27
  27.1 13.0 %collective-permute-start.5 = (bf16[64,1152]{1,0:T(8,128)(2,1)S(1)}, bf16[64,1152]{1,0:T(8,128)(2,1)S(1)}, u32[]{:S(2)}, u32[]{:S(2)}) collective-permute-start(bf16[64,1152]{1,0:T(8,128)(2,1)S(1)} %maximum_select_fusion.11), channel_id=1, source_target_pairs={{0,2},{2,4},{4,6},{6,0},{1,3},{3,5},{5,7},{7,1},{8,10},{10,12},{12... | collective-permute-start | bytes 442376 | tf_op jit(solution)/shard_map/ppermute | solution.py:27
  40.2 13.2 %collective-permute-start.13 = (bf16[2,128,1024]{2,1,0:T(8,128)(2,1)}, bf16[2,128,1024]{2,1,0:T(8,128)(2,1)S(1)}, u32[]{:S(2)}, u32[]{:S(2)}) collective-permute-start(bf16[2,128,1024]{2,1,0:T(8,128)(2,1)} %bitcast.13), channel_id=1, source_target_pairs={{0,32},{32,0},{1,33},{33,1},{2,34},{34,2},{3,35},{35,3},{4,36},{36... | collective-permute-start | bytes 1572872 | tf_op jit(solution)/shard_map/ppermute | solution.py:27
  40.7 12.7 %collective-permute-start.12 = (bf16[2,256,1024]{2,1,0:T(8,128)(2,1)S(1)}, bf16[2,256,1024]{2,1,0:T(8,128)(2,1)S(1)}, u32[]{:S(2)}, u32[]{:S(2)}) collective-permute-start(bf16[2,256,1024]{2,1,0:T(8,128)(2,1)S(1)} %maximum_select_fusion), channel_id=1, source_target_pairs={{0,1},{1,0},{2,3},{3,2},{4,5},{5,4},{6,7},{7,6},{8,9},{9,8},{10,11... | collective-permute-start | bytes 3145736 | tf_op jit(solution)/shard_map/ppermute | solution.py:27
  41.0 8.5 %collective-permute-start.10 = (bf16[64,1152]{1,0:T(8,128)(2,1)S(1)}, bf16[64,1152]{1,0:T(8,128)(2,1)S(1)}, u32[]{:S(2)}, u32[]{:S(2)}) collective-permute-start(bf16[64,1152]{1,0:T(8,128)(2,1)S(1)} %pad_maximum_fusion.7), channel_id=1, source_target_pairs={{0,16},{8,24},{16,0},{24,8},{1,17},{9,25},{17,1},{25,9},{2,18},{10... | collective-permute-start | bytes 442376 | tf_op jit(solution)/shard_map/ppermute | solution.py:27
  44.4 8.0 %collective-permute-start.9 = (bf16[64,1152]{1,0:T(8,128)(2,1)S(1)}, bf16[64,1152]{1,0:T(8,128)(2,1)S(1)}, u32[]{:S(2)}, u32[]{:S(2)}) collective-permute-start(bf16[64,1152]{1,0:T(8,128)(2,1)S(1)} %pad_maximum_fusion.7), channel_id=1, source_target_pairs={{0,8},{8,16},{16,24},{24,0},{1,9},{9,17},{17,25},{25,1},{2,10},{10... | collective-permute-start | bytes 442376 | tf_op jit(solution)/shard_map/ppermute | solution.py:27
  45.1 8.2 %collective-permute-start.11 = (bf16[64,1152]{1,0:T(8,128)(2,1)S(1)}, bf16[64,1152]{1,0:T(8,128)(2,1)S(1)}, u32[]{:S(2)}, u32[]{:S(2)}) collective-permute-start(bf16[64,1152]{1,0:T(8,128)(2,1)S(1)} %pad_maximum_fusion.7), channel_id=1, source_target_pairs={{0,24},{8,0},{16,8},{24,16},{1,25},{9,1},{17,9},{25,17},{2,26},{10... | collective-permute-start | bytes 442376 | tf_op jit(solution)/shard_map/ppermute | solution.py:27
  89.1 2.1 collective-permute-start.14
  91.4 10.4 %collective-permute-start.15 = (bf16[128,1024]{1,0:T(8,128)(2,1)S(1)}, bf16[128,1024]{1,0:T(8,128)(2,1)S(1)}, u32[]{:S(2)}, u32[]{:S(2)}) collective-permute-start(bf16[128,1024]{1,0:T(8,128)(2,1)S(1)} %fusion.24), channel_id=1, source_target_pairs={{0,32},{32,0},{1,33},{33,1},{2,34},{34,2},{3,35},{35,3},{4,36},{36... | collective-permute-start | bytes 786440 | tf_op jit(solution)/shard_map/ppermute | solution.py:27
  101.9 3.2 collective-permute-start.18
  104.6 23.2 %collective-permute-start.22 = (bf16[2,256,1024]{2,1,0:T(8,128)(2,1)}, bf16[2,256,1024]{2,1,0:T(8,128)(2,1)}, u32[]{:S(2)}, u32[]{:S(2)}) collective-permute-start(bf16[2,256,1024]{2,1,0:T(8,128)(2,1)} %maximum_select_fusion.1), channel_id=1, source_target_pairs={{0,1},{1,0},{2,3},{3,2},{4,5},{5,4},{6,7},{7,6},{8,9},{9,8},{10,11... | collective-permute-start | bytes 3145736 | tf_op jit(solution)/shard_map/ppermute | solution.py:27
  107.4 9.2 %collective-permute-start.19 = (bf16[128,1024]{1,0:T(8,128)(2,1)S(1)}, bf16[128,1024]{1,0:T(8,128)(2,1)S(1)}, u32[]{:S(2)}, u32[]{:S(2)}) collective-permute-start(bf16[128,1024]{1,0:T(8,128)(2,1)S(1)} %fusion.25), channel_id=1, source_target_pairs={{0,32},{32,0},{1,33},{33,1},{2,34},{34,2},{3,35},{35,3},{4,36},{36... | collective-permute-start | bytes 786440 | tf_op jit(solution)/shard_map/ppermute | solution.py:27
  107.9 14.0 %collective-permute-start.17 = (bf16[128,1024]{1,0:T(8,128)(2,1)S(1)}, bf16[128,1024]{1,0:T(8,128)(2,1)S(1)}, u32[]{:S(2)}, u32[]{:S(2)}) collective-permute-start(bf16[128,1024]{1,0:T(8,128)(2,1)S(1)} %fusion.19), channel_id=1, source_target_pairs={{0,96},{32,64},{64,32},{96,0},{1,97},{33,65},{65,33},{97,1},{2,98}... | collective-permute-start | bytes 786440 | tf_op jit(solution)/shard_map/ppermute | solution.py:754
  110.9 12.1 %collective-permute-start.16 = (bf16[128,1024]{1,0:T(8,128)(2,1)S(1)}, bf16[128,1024]{1,0:T(8,128)(2,1)}, u32[]{:S(2)}, u32[]{:S(2)}) collective-permute-start(bf16[128,1024]{1,0:T(8,128)(2,1)S(1)} %fusion.19), channel_id=1, source_target_pairs={{0,64},{32,96},{64,0},{96,32},{1,65},{33,97},{65,1},{97,33},{2,66}... | collective-permute-start | bytes 786440 | tf_op jit(solution)/shard_map/ppermute | solution.py:753
  125.4 7.4 %collective-permute-start.23 = (bf16[256,1024]{1,0:T(8,128)(2,1)S(1)}, bf16[256,1024]{1,0:T(8,128)(2,1)S(1)}, u32[]{:S(2)}, u32[]{:S(2)}) collective-permute-start(bf16[256,1024]{1,0:T(8,128)(2,1)S(1)} %get-tuple-element.256.refs_0_.refs_14_), channel_id=1, source_target_pairs={{0,1},{1,0},{2,3},{3,2},{4,5},{5,4},{6,7},{7,6},{8,9},{9,8},{10,11... | collective-permute-start | bytes 1572872 | tf_op jit(solution)/shard_map/ppermute | solution.py:27
  129.1 23.2 %collective-permute-start.21 = (bf16[128,1024]{1,0:T(8,128)(2,1)S(1)}, bf16[128,1024]{1,0:T(8,128)(2,1)S(1)}, u32[]{:S(2)}, u32[]{:S(2)}) collective-permute-start(bf16[128,1024]{1,0:T(8,128)(2,1)S(1)} %fusion.16), channel_id=1, source_target_pairs={{0,96},{32,64},{64,32},{96,0},{1,97},{33,65},{65,33},{97,1},{2,98}... | collective-permute-start | bytes 786440 | tf_op jit(solution)/shard_map/ppermute | solution.py:754
  132.6 19.8 %collective-permute-start.20 = (bf16[128,1024]{1,0:T(8,128)(2,1)S(1)}, bf16[128,1024]{1,0:T(8,128)(2,1)S(1)}, u32[]{:S(2)}, u32[]{:S(2)}) collective-permute-start(bf16[128,1024]{1,0:T(8,128)(2,1)S(1)} %fusion.16), channel_id=1, source_target_pairs={{0,64},{32,96},{64,0},{96,32},{1,65},{33,97},{65,1},{97,33},{2,66}... | collective-permute-start | bytes 786440 | tf_op jit(solution)/shard_map/ppermute | solution.py:753
  152.3 3.3 collective-permute-start.24
  154.2 2.8 collective-permute-start.26
  155.9 10.2 %collective-permute-start.25 = (bf16[128,1024]{1,0:T(8,128)(2,1)S(1)}, bf16[128,1024]{1,0:T(8,128)(2,1)S(1)}, u32[]{:S(2)}, u32[]{:S(2)}) collective-permute-start(bf16[128,1024]{1,0:T(8,128)(2,1)S(1)} %fusion.26), channel_id=1, source_target_pairs={{0,32},{32,0},{1,33},{33,1},{2,34},{34,2},{3,35},{35,3},{4,36},{36... | collective-permute-start | bytes 786440 | tf_op jit(solution)/shard_map/ppermute | solution.py:27
  166.2 15.2 %collective-permute-start.28 = (bf16[128,1024]{1,0:T(8,128)(2,1)S(1)}, bf16[128,1024]{1,0:T(8,128)(2,1)S(1)}, u32[]{:S(2)}, u32[]{:S(2)}) collective-permute-start(bf16[128,1024]{1,0:T(8,128)(2,1)S(1)} %fusion.13), channel_id=1, source_target_pairs={{0,96},{32,64},{64,32},{96,0},{1,97},{33,65},{65,33},{97,1},{2,98}... | collective-permute-start | bytes 786440 | tf_op jit(solution)/shard_map/ppermute | solution.py:754
  169.4 12.0 %collective-permute-start.27 = (bf16[128,1024]{1,0:T(8,128)(2,1)S(1)}, bf16[128,1024]{1,0:T(8,128)(2,1)S(1)}, u32[]{:S(2)}, u32[]{:S(2)}) collective-permute-start(bf16[128,1024]{1,0:T(8,128)(2,1)S(1)} %fusion.13), channel_id=1, source_target_pairs={{0,64},{32,96},{64,0},{96,32},{1,65},{33,97},{65,1},{97,33},{2,66}... | collective-permute-start | bytes 786440 | tf_op jit(solution)/shard_map/ppermute | solution.py:753
  182.9 3.3 collective-permute-start.29
  185.5 13.8 %collective-permute-start.33 = (bf16[256,1024]{1,0:T(8,128)(2,1)S(1)}, bf16[256,1024]{1,0:T(8,128)(2,1)S(1)}, u32[]{:S(2)}, u32[]{:S(2)}) collective-permute-start(bf16[256,1024]{1,0:T(8,128)(2,1)S(1)} %get-tuple-element.201.refs_0_.refs_2_.refs_6_), channel_id=1, source_target_pairs={{0,1},{1,0},{2,3},{3,2},{4,5},{5,4},{6,7},{7,6},{8,9},{9,8},{10,11... | collective-permute-start | bytes 1572872 | tf_op jit(solution)/shard_map/ppermute | solution.py:27
  187.9 8.1 %collective-permute-start.30 = (bf16[128,1024]{1,0:T(8,128)(2,1)S(1)}, bf16[128,1024]{1,0:T(8,128)(2,1)S(1)}, u32[]{:S(2)}, u32[]{:S(2)}) collective-permute-start(bf16[128,1024]{1,0:T(8,128)(2,1)S(1)} %fusion.27), channel_id=1, source_target_pairs={{0,32},{32,0},{1,33},{33,1},{2,34},{34,2},{3,35},{35,3},{4,36},{36... | collective-permute-start | bytes 786440 | tf_op jit(solution)/shard_map/ppermute | solution.py:27
  196.1 14.0 %collective-permute-start.32 = (bf16[128,1024]{1,0:T(8,128)(2,1)S(1)}, bf16[128,1024]{1,0:T(8,128)(2,1)S(1)}, u32[]{:S(2)}, u32[]{:S(2)}) collective-permute-start(bf16[128,1024]{1,0:T(8,128)(2,1)S(1)} %fusion.10), channel_id=1, source_target_pairs={{0,96},{32,64},{64,32},{96,0},{1,97},{33,65},{65,33},{97,1},{2,98}... | collective-permute-start | bytes 786440 | tf_op jit(solution)/shard_map/ppermute | solution.py:754
  199.1 11.0 %collective-permute-start.31 = (bf16[128,1024]{1,0:T(8,128)(2,1)S(1)}, bf16[128,1024]{1,0:T(8,128)(2,1)S(1)}, u32[]{:S(2)}, u32[]{:S(2)}) collective-permute-start(bf16[128,1024]{1,0:T(8,128)(2,1)S(1)} %fusion.10), channel_id=1, source_target_pairs={{0,64},{32,96},{64,0},{96,32},{1,65},{33,97},{65,1},{97,33},{2,66}... | collective-permute-start | bytes 786440 | tf_op jit(solution)/shard_map/ppermute | solution.py:753
  212.8 1.9 collective-permute-start.34
  216.1 24.2 %collective-permute-start.35 = (bf16[3,256,1024]{2,1,0:T(8,128)(2,1)}, bf16[3,256,1024]{2,1,0:T(8,128)(2,1)}, u32[]{:S(2)}, u32[]{:S(2)}) collective-permute-start(bf16[3,256,1024]{2,1,0:T(8,128)(2,1)} %pad_maximum_fusion), channel_id=1, source_target_pairs={{0,1},{1,0},{2,3},{3,2},{4,5},{5,4},{6,7},{7,6},{8,9},{9,8},{10,11... | collective-permute-start | bytes 4718600 | tf_op jit(solution)/shard_map/ppermute | solution.py:27
  233.4 3.9 %collective-permute-start.40 = (f32[8,1024]{1,0:T(8,128)S(1)}, f32[8,1024]{1,0:T(8,128)S(1)}, u32[]{:S(2)}, u32[]{:S(2)}) collective-permute-start(f32[8,1024]{1,0:T(8,128)S(1)} %add.453), channel_id=1, source_target_pairs={{0,8},{8,0},{16,24},{24,16},{1,9},{9,1},{17,25},{25,17},{2,10},{10... | collective-permute-start | bytes 98312 | tf_op jit(solution)/shard_map/ppermute | solution.py:44
  234.8 29.2 %collective-permute-start.43 = (bf16[256,1024]{1,0:T(8,128)(2,1)}, bf16[256,1024]{1,0:T(8,128)(2,1)S(1)}, u32[]{:S(2)}, u32[]{:S(2)}) collective-permute-start(bf16[256,1024]{1,0:T(8,128)(2,1)} %get-tuple-element.210), channel_id=1, source_target_pairs={{0,1},{1,0},{2,3},{3,2},{4,5},{5,4},{6,7},{7,6},{8,9},{9,8},{10,11... | collective-permute-start | bytes 1572872 | tf_op jit(solution)/shard_map/ppermute | solution.py:27
  237.3 25.5 %collective-permute-start.41 = (f32[8,1024]{1,0:T(8,128)S(1)}, f32[8,1024]{1,0:T(8,128)S(1)}, u32[]{:S(2)}, u32[]{:S(2)}) collective-permute-start(f32[8,1024]{1,0:T(8,128)S(1)} %add.454), channel_id=1, source_target_pairs={{0,16},{8,24},{16,0},{24,8},{1,17},{9,25},{17,1},{25,9},{2,18},{10... | collective-permute-start | bytes 98312 | tf_op jit(solution)/shard_map/ppermute | solution.py:44
  245.0 26.9 %collective-permute-start.42 = (bf16[3,128,1024]{2,1,0:T(8,128)(2,1)}, bf16[3,128,1024]{2,1,0:T(8,128)(2,1)}, u32[]{:S(2)}, u32[]{:S(2)}) collective-permute-start(bf16[3,128,1024]{2,1,0:T(8,128)(2,1)} %fusion.6), channel_id=1, source_target_pairs={{0,32},{32,0},{1,33},{33,1},{2,34},{34,2},{3,35},{35,3},{4,36},{36... | collective-permute-start | bytes 2359304 | tf_op jit(solution)/shard_map/ppermute | solution.py:27
  259.7 7.5 %collective-permute-start.37 = (bf16[4,64,512]{2,0,1:T(4,128)(2,1)}, bf16[4,64,512]{2,0,1:T(4,128)(2,1)S(1)}, u32[]{:S(2)}, u32[]{:S(2)}) collective-permute-start(bf16[4,64,512]{2,0,1:T(4,128)(2,1)} %get-tuple-element.285), channel_id=1, source_target_pairs={{0,24},{8,0},{16,8},{24,16},{1,25},{9,1},{17,9},{25,17},{2,26},{10... | collective-permute-start | bytes 786440 | tf_op jit(solution)/shard_map/ppermute | solution.py:27
  260.8 8.1 %collective-permute-start.36 = (bf16[4,64,512]{2,0,1:T(4,128)(2,1)}, bf16[4,64,512]{2,0,1:T(4,128)(2,1)}, u32[]{:S(2)}, u32[]{:S(2)}) collective-permute-start(bf16[4,64,512]{2,0,1:T(4,128)(2,1)} %get-tuple-element.286), channel_id=1, source_target_pairs={{0,8},{8,16},{16,24},{24,0},{1,9},{9,17},{17,25},{25,1},{2,10},{10... | collective-permute-start | bytes 786440 | tf_op jit(solution)/shard_map/ppermute | solution.py:27
  262.8 6.7 %collective-permute-start.39 = (bf16[4,64,512]{2,1,0:T(8,128)(2,1)}, bf16[4,64,512]{2,1,0:T(8,128)(2,1)}, u32[]{:S(2)}, u32[]{:S(2)}) collective-permute-start(bf16[4,64,512]{2,1,0:T(8,128)(2,1)} %get-tuple-element.283), channel_id=1, source_target_pairs={{0,6},{2,0},{4,2},{6,4},{1,7},{3,1},{5,3},{7,5},{8,14},{10,8},{12,... | collective-permute-start | bytes 786440 | tf_op jit(solution)/shard_map/ppermute | solution.py:27
  264.0 7.9 %collective-permute-start.38 = (bf16[4,64,512]{2,1,0:T(8,128)(2,1)}, bf16[4,64,512]{2,1,0:T(8,128)(2,1)}, u32[]{:S(2)}, u32[]{:S(2)}) collective-permute-start(bf16[4,64,512]{2,1,0:T(8,128)(2,1)} %get-tuple-element.284), channel_id=1, source_target_pairs={{0,2},{2,4},{4,6},{6,0},{1,3},{3,5},{5,7},{7,1},{8,10},{10,12},{12... | collective-permute-start | bytes 786440 | tf_op jit(solution)/shard_map/ppermute | solution.py:27
  275.2 7.7 %collective-permute-start.48 = (f32[8,1024]{1,0:T(8,128)S(1)}, f32[8,1024]{1,0:T(8,128)S(1)}, u32[]{:S(2)}, u32[]{:S(2)}) collective-permute-start(f32[8,1024]{1,0:T(8,128)S(1)} %add.467), channel_id=1, source_target_pairs={{0,2},{2,0},{4,6},{6,4},{1,3},{3,1},{5,7},{7,5},{8,10},{10,8},{12,... | collective-permute-start | bytes 98312 | tf_op jit(solution)/shard_map/ppermute | solution.py:44
  275.5 14.4 %collective-permute-start.44 = (bf16[4,64,1024]{2,0,1:T(4,128)(2,1)S(1)}, bf16[4,64,1024]{2,0,1:T(4,128)(2,1)S(1)}, u32[]{:S(2)}, u32[]{:S(2)}) collective-permute-start(bf16[4,64,1024]{2,0,1:T(4,128)(2,1)S(1)} %pad_maximum_fusion.1), channel_id=1, source_target_pairs={{0,8},{8,16},{16,24},{24,0},{1,9},{9,17},{17,25},{25,1},{2,10},{10... | collective-permute-start | bytes 1572872 | tf_op jit(solution)/shard_map/ppermute | solution.py:27
  276.1 13.9 %collective-permute-start.45 = (bf16[4,64,1024]{2,0,1:T(4,128)(2,1)S(1)}, bf16[4,64,1024]{2,0,1:T(4,128)(2,1)S(1)}, u32[]{:S(2)}, u32[]{:S(2)}) collective-permute-start(bf16[4,64,1024]{2,0,1:T(4,128)(2,1)S(1)} %pad_maximum_fusion.2), channel_id=1, source_target_pairs={{0,24},{8,0},{16,8},{24,16},{1,25},{9,1},{17,9},{25,17},{2,26},{10... | collective-permute-start | bytes 1572872 | tf_op jit(solution)/shard_map/ppermute | solution.py:27
  279.2 14.0 %collective-permute-start.46 = (bf16[4,64,1024]{2,1,0:T(8,128)(2,1)S(1)}, bf16[4,64,1024]{2,1,0:T(8,128)(2,1)S(1)}, u32[]{:S(2)}, u32[]{:S(2)}) collective-permute-start(bf16[4,64,1024]{2,1,0:T(8,128)(2,1)S(1)} %pad_maximum_fusion.3), channel_id=1, source_target_pairs={{0,2},{2,4},{4,6},{6,0},{1,3},{3,5},{5,7},{7,1},{8,10},{10,12},{12... | collective-permute-start | bytes 1572872 | tf_op jit(solution)/shard_map/ppermute | solution.py:27
  281.3 12.7 %collective-permute-start.47 = (bf16[4,64,1024]{2,1,0:T(8,128)(2,1)S(1)}, bf16[4,64,1024]{2,1,0:T(8,128)(2,1)S(1)}, u32[]{:S(2)}, u32[]{:S(2)}) collective-permute-start(bf16[4,64,1024]{2,1,0:T(8,128)(2,1)S(1)} %pad_maximum_fusion.4), channel_id=1, source_target_pairs={{0,6},{2,0},{4,2},{6,4},{1,7},{3,1},{5,3},{7,5},{8,14},{10,8},{12,... | collective-permute-start | bytes 1572872 | tf_op jit(solution)/shard_map/ppermute | solution.py:27
  282.9 6.7 %collective-permute-start.49 = (bf16[128,1024]{1,0:T(8,128)(2,1)S(1)}, bf16[128,1024]{1,0:T(8,128)(2,1)S(1)}, u32[]{:S(2)}, u32[]{:S(2)}) collective-permute-start(bf16[128,1024]{1,0:T(8,128)(2,1)S(1)} %fusion.28), channel_id=1, source_target_pairs={{0,32},{32,0},{1,33},{33,1},{2,34},{34,2},{3,35},{35,3},{4,36},{36... | collective-permute-start | bytes 786440 | tf_op jit(solution)/shard_map/ppermute | solution.py:27
  294.9 8.6 %collective-permute-start.56 = (f32[8,1024]{1,0:T(8,128)S(1)}, f32[8,1024]{1,0:T(8,128)S(1)}, u32[]{:S(2)}, u32[]{:S(2)}) collective-permute-start(f32[8,1024]{1,0:T(8,128)S(1)} %add.482), channel_id=1, source_target_pairs={{0,4},{2,6},{4,0},{6,2},{1,5},{3,7},{5,1},{7,3},{8,12},{10,14},{12... | collective-permute-start | bytes 98312 | tf_op jit(solution)/shard_map/ppermute | solution.py:44
  297.3 6.9 %collective-permute-start.55 = (bf16[64,1024]{1,0:T(8,128)(2,1)S(1)}, bf16[64,1024]{1,0:T(8,128)(2,1)S(1)}, u32[]{:S(2)}, u32[]{:S(2)}) collective-permute-start(bf16[64,1024]{1,0:T(8,128)(2,1)S(1)} %get-tuple-element.280), channel_id=1, source_target_pairs={{0,16},{8,24},{16,0},{24,8},{1,17},{9,25},{17,1},{25,9},{2,18},{10... | collective-permute-start | bytes 393224 | tf_op jit(solution)/shard_map/ppermute | solution.py:27
  299.0 8.8 %collective-permute-start.54 = (bf16[64,1024]{1,0:T(8,128)(2,1)S(1)}, bf16[64,1024]{1,0:T(8,128)(2,1)S(1)}, u32[]{:S(2)}, u32[]{:S(2)}) collective-permute-start(bf16[64,1024]{1,0:T(8,128)(2,1)S(1)} %get-tuple-element.281), channel_id=1, source_target_pairs={{0,24},{8,0},{16,8},{24,16},{1,25},{9,1},{17,9},{25,17},{2,26},{10... | collective-permute-start | bytes 393224 | tf_op jit(solution)/shard_map/ppermute | solution.py:27
  299.8 8.0 %collective-permute-start.53 = (bf16[64,1024]{1,0:T(8,128)(2,1)S(1)}, bf16[64,1024]{1,0:T(8,128)(2,1)S(1)}, u32[]{:S(2)}, u32[]{:S(2)}) collective-permute-start(bf16[64,1024]{1,0:T(8,128)(2,1)S(1)} %get-tuple-element.282), channel_id=1, source_target_pairs={{0,8},{8,16},{16,24},{24,0},{1,9},{9,17},{17,25},{25,1},{2,10},{10... | collective-permute-start | bytes 393224 | tf_op jit(solution)/shard_map/ppermute | solution.py:27
  301.2 8.3 %collective-permute-start.52 = (bf16[64,1792]{1,0:T(8,128)(2,1)S(1)}, bf16[64,1792]{1,0:T(8,128)(2,1)S(1)}, u32[]{:S(2)}, u32[]{:S(2)}) collective-permute-start(bf16[64,1792]{1,0:T(8,128)(2,1)S(1)} %get-tuple-element.277), channel_id=1, source_target_pairs={{0,4},{2,6},{4,0},{6,2},{1,5},{3,7},{5,1},{7,3},{8,12},{10,14},{12... | collective-permute-start | bytes 688136 | tf_op jit(solution)/shard_map/ppermute | solution.py:27
  303.5 9.1 %collective-permute-start.50 = (bf16[64,1792]{1,0:T(8,128)(2,1)S(1)}, bf16[64,1792]{1,0:T(8,128)(2,1)S(1)}, u32[]{:S(2)}, u32[]{:S(2)}) collective-permute-start(bf16[64,1792]{1,0:T(8,128)(2,1)S(1)} %get-tuple-element.278), channel_id=1, source_target_pairs={{0,2},{2,4},{4,6},{6,0},{1,3},{3,5},{5,7},{7,1},{8,10},{10,12},{12... | collective-permute-start | bytes 688136 | tf_op jit(solution)/shard_map/ppermute | solution.py:27
  304.1 8.5 %collective-permute-start.51 = (bf16[64,1792]{1,0:T(8,128)(2,1)S(1)}, bf16[64,1792]{1,0:T(8,128)(2,1)S(1)}, u32[]{:S(2)}, u32[]{:S(2)}) collective-permute-start(bf16[64,1792]{1,0:T(8,128)(2,1)S(1)} %get-tuple-element.279), channel_id=1, source_target_pairs={{0,6},{2,0},{4,2},{6,4},{1,7},{3,1},{5,3},{7,5},{8,14},{10,8},{12,... | collective-permute-start | bytes 688136 | tf_op jit(solution)/shard_map/ppermute | solution.py:27
  312.8 1.3 collective-permute-start.58
  313.0 1.6 collective-permute-start.57
  314.7 30.9 %collective-permute-start.60 = (bf16[32,1024]{1,0:T(8,128)(2,1)S(1)}, bf16[32,1024]{1,0:T(8,128)(2,1)S(1)}, u32[]{:S(2)}, u32[]{:S(2)}) collective-permute-start(bf16[32,1024]{1,0:T(8,128)(2,1)S(1)} %add_convert_fusion.4.out_own), channel_id=1, source_target_pairs={{0,32},{32,0},{1,33},{33,1},{2,34},{34,2},{3,35},{35,3},{4,36},{36... | collective-permute-start | bytes 196616 | tf_op jit(solution)/shard_map/ppermute | solution.py:27
  316.0 29.5 %collective-permute-start.61 = (f32[2,8,1024]{2,1,0:T(8,128)S(1)}, f32[2,8,1024]{2,1,0:T(8,128)S(1)}, u32[]{:S(2)}, u32[]{:S(2)}) collective-permute-start(f32[2,8,1024]{2,1,0:T(8,128)S(1)} %maximum_select_fusion.14), channel_id=1, source_target_pairs={{0,32},{32,0},{1,33},{33,1},{2,34},{34,2},{3,35},{35,3},{4,36},{36... | collective-permute-start | bytes 196616 | tf_op jit(solution)/shard_map/ppermute | solution.py:27
  317.0 28.6 %collective-permute-start.59 = (bf16[64,1792]{1,0:T(8,128)(2,1)S(1)}, bf16[64,1792]{1,0:T(8,128)(2,1)S(1)}, u32[]{:S(2)}, u32[]{:S(2)}) collective-permute-start(bf16[64,1792]{1,0:T(8,128)(2,1)S(1)} %maximum_select_fusion.10), channel_id=1, source_target_pairs={{0,32},{32,0},{1,33},{33,1},{2,34},{34,2},{3,35},{35,3},{4,36},{36... | collective-permute-start | bytes 688136 | tf_op jit(solution)/shard_map/ppermute | solution.py:27
  344.0 5.2 %collective-permute-start.62 = (bf16[64,1024]{1,0:T(8,128)(2,1)}, bf16[64,1024]{1,0:T(8,128)(2,1)S(1)}, u32[]{:S(2)}, u32[]{:S(2)}) collective-permute-start(bf16[64,1024]{1,0:T(8,128)(2,1)} %reduce-scatter.2.cloned.1.call-done), channel_id=1, source_target_pairs={{0,32},{32,0},{1,33},{33,1},{2,34},{34,2},{3,35},{35,3},{4,36},{36... | collective-permute-start | bytes 393224 | tf_op jit(solution)/shard_map/ppermute | solution.py:27
  (112 other events, 1311.4 us)
Sparse Core Ops, SparseCore 0:
  12.4 65.2 all-gather.1
  265.2 78.6 reduce-scatter.1
